TPU v7x, 128 devices: a whole 4x4x4 slice. The times are simulated.
128 devices in a mesh: expert: 64 (over z, y, x), tensor: 2 (over core).
Axes of the slice: x: 4, y: 4, z: 4, core: 2. Of those that a mesh axis runs over, the one named last changes fastest.
Arguments:
- tokens: bfloat16 [2048, 4096], P('expert', 'tensor'), may hold values from -6 to 6
- route_ids: int32 [2048, 8], P('expert'), may hold values from 0 to 63, all different within a row; in each aligned block of 32 rows (0 to 31, 32 to 63, ...) at most 8 rows name the same one
- route_weight: float32 [2048, 8], P('expert'), may hold values from 0.05 to 0.5
- gate_weight: bfloat16 [64, 768, 4096], P('expert', 'tensor'), may hold values from -0.09375 to 0.09375
- up_weight: bfloat16 [64, 768, 4096], P('expert', 'tensor'), may hold values from -0.09375 to 0.09375
- down_weight: bfloat16 [64, 768, 4096], P('expert', 'tensor'), may hold values from -0.21875 to 0.21875
- out_grad: bfloat16 [2048, 4096], P('expert', 'tensor'), may hold values from -6 to 6
Outputs:
- mixed: bfloat16 [2048, 4096], P('expert', 'tensor')
- tokens_grad: bfloat16 [2048, 4096], P('expert', 'tensor')
- route_grad: float32 [2048, 8], P('expert')
- gate_grad: bfloat16 [64, 768, 4096], P('expert', 'tensor')
- up_grad: bfloat16 [64, 768, 4096], P('expert', 'tensor')
- down_grad: bfloat16 [64, 768, 4096], P('expert', 'tensor')
Inputs may be any that keep to these rules, and one draw needn't show every extreme that they name: `route_ids`: each row names 8 different experts. Within each aligned block of 32 rows (the tokens of one index of expert) no expert is named by more than 8 rows.
All inputs are finite; a program needn't handle non-finite values.
Results may differ from a plain program's by a relative error of at most 0.015.
Values may be sent and summed in bfloat16 or wider, within the bound.
A program may use at most 128 MiB of HBM per device.

v0:
```python
import jax
import jax.numpy as jnp
from jax import lax
from jax.sharding import PartitionSpec as P


def contract_rows(left, right):
    return lax.dot_general(
        left, right, (((0,), (0,)), ((), ())), preferred_element_type=jnp.float32
    )


def contract_cols(left, right):
    return lax.dot_general(
        left, right, (((1,), (1,)), ((), ())), preferred_element_type=jnp.float32
    )


def shards(tokens, route_ids, route_weight, gate_weight, up_weight, down_weight, out_grad):
    tok_count = tokens.shape[0]
    local_width = tokens.shape[1]
    top_count = route_ids.shape[1]
    groups_count = lax.axis_size("expert")
    tensor_count = lax.axis_size("tensor")
    experts = gate_weight.shape[0] * groups_count
    capacity = 2 * tok_count * top_count // experts
    slot_count = groups_count * capacity
    gate_mat = gate_weight[0]
    up_mat = up_weight[0]
    down_mat = down_weight[0]
    hidden_width = gate_mat.shape[0]
    model_width = gate_mat.shape[1]
    flat_ids = route_ids.reshape(-1)
    expert_hits = (flat_ids[:, None] == jnp.arange(experts, dtype=jnp.int32)[None, :]).astype(
        jnp.int32
    )
    position = jnp.sum((jnp.cumsum(expert_hits, axis=0) - 1) * expert_hits, axis=1)
    slot_index = flat_ids * capacity + position
    slot_table = slot_index[:, None] == jnp.arange(experts * capacity, dtype=jnp.int32)[None, :]
    send_rows = contract_rows(
        slot_table.astype(jnp.bfloat16), jnp.repeat(tokens, top_count, axis=0)
    ).astype(jnp.bfloat16)
    received = lax.all_to_all(
        send_rows.reshape(experts, capacity, local_width),
        "expert",
        split_axis=0,
        concat_axis=0,
        tiled=True,
    )
    token_rows = lax.all_gather(received, "tensor", axis=2, tiled=True).reshape(
        slot_count, model_width
    )
    gate_act = contract_cols(token_rows, gate_mat)
    up_act = contract_cols(token_rows, up_mat)
    sigmoid_gate = jax.nn.sigmoid(gate_act)
    swish = gate_act * sigmoid_gate
    hidden = (swish * up_act).astype(jnp.bfloat16)
    partial_out = jnp.dot(hidden, down_mat, preferred_element_type=jnp.float32)
    local_out = lax.psum_scatter(
        partial_out.astype(jnp.bfloat16), "tensor", scatter_dimension=1, tiled=True
    )
    returned = lax.all_to_all(
        local_out.reshape(groups_count, capacity, local_width),
        "expert",
        split_axis=0,
        concat_axis=0,
        tiled=True,
    )
    picked = (
        jnp.take(returned.reshape(experts * capacity, local_width), slot_index, axis=0)
        .astype(jnp.float32)
        .reshape(tok_count, top_count, local_width)
    )
    mixed = jnp.sum(route_weight[:, :, None] * picked, axis=1).astype(jnp.bfloat16)
    grad_float = out_grad.astype(jnp.float32)
    route_part = jnp.sum(picked * grad_float[:, None, :], axis=2)
    route_grad = lax.psum(route_part, "tensor")
    weighted = route_weight.reshape(-1)[:, None] * jnp.repeat(grad_float, top_count, axis=0)
    send_grads = lax.dot_general(
        slot_table.astype(jnp.float32),
        weighted,
        (((0,), (0,)), ((), ())),
        precision=lax.Precision.HIGHEST,
        preferred_element_type=jnp.float32,
    ).astype(jnp.bfloat16)
    grad_received = lax.all_to_all(
        send_grads.reshape(experts, capacity, local_width),
        "expert",
        split_axis=0,
        concat_axis=0,
        tiled=True,
    )
    slot_rows = lax.all_gather(grad_received, "tensor", axis=2, tiled=True).reshape(
        slot_count, model_width
    )
    hidden_grad = contract_cols(slot_rows, down_mat)
    gate_delta = (
        hidden_grad * up_act * sigmoid_gate * (1.0 + gate_act * (1.0 - sigmoid_gate))
    ).astype(jnp.bfloat16)
    up_delta = (hidden_grad * swish).astype(jnp.bfloat16)
    gate_cols, up_cols = (
        lax.all_to_all(gate_mat, "tensor", split_axis=1, concat_axis=0, tiled=True),
        lax.all_to_all(up_mat, "tensor", split_axis=1, concat_axis=0, tiled=True),
    )
    paired_cols = jnp.stack(
        [
            gate_cols.reshape(tensor_count, hidden_width, local_width),
            up_cols.reshape(tensor_count, hidden_width, local_width),
        ],
        axis=1,
    )
    paired_deltas = jnp.concatenate([gate_delta, up_delta], axis=1)
    portion = lax.all_gather(paired_deltas, "tensor", axis=1, tiled=True)
    group_total = portion.shape[1] // (2 * hidden_width)
    products = jnp.einsum(
        "skcf,kcfd->ksd",
        portion.reshape(slot_count, group_total, 2, hidden_width),
        paired_cols,
        preferred_element_type=jnp.float32,
    )
    rounded = lax.optimization_barrier(products.astype(jnp.bfloat16)).astype(jnp.float32)
    local_back = jnp.sum(rounded, axis=0).astype(jnp.bfloat16)
    back_home = lax.all_to_all(
        local_back.reshape(groups_count, capacity, local_width),
        "expert",
        split_axis=0,
        concat_axis=0,
        tiled=True,
    )
    gathered_back = (
        jnp.take(back_home.reshape(experts * capacity, local_width), slot_index, axis=0)
        .astype(jnp.float32)
        .reshape(tok_count, top_count, local_width)
    )
    tokens_grad = jnp.sum(gathered_back, axis=1).astype(jnp.bfloat16)
    gate_grad = contract_rows(gate_delta, token_rows).astype(jnp.bfloat16)
    up_grad = contract_rows(up_delta, token_rows).astype(jnp.bfloat16)
    down_grad = contract_rows(hidden, slot_rows).astype(jnp.bfloat16)
    return (mixed, tokens_grad, route_grad, gate_grad[None], up_grad[None], down_grad[None])


def solution(mesh):
    placed = (
        P("expert", "tensor"),
        P("expert", None),
        P("expert", None),
        P("expert", "tensor", None),
        P("expert", "tensor", None),
        P("expert", "tensor", None),
        P("expert", "tensor"),
    )
    return jax.shard_map(
        shards,
        mesh=mesh,
        in_specs=placed,
        out_specs=(
            P("expert", "tensor"),
            P("expert", "tensor"),
            P("expert", None),
            P("expert", "tensor", None),
            P("expert", "tensor", None),
            P("expert", "tensor", None),
        ),
        check_vma=False,
    )
```

profile of v0, /device:TPU:1, one launch (start us, length us, event | category | flops | bytes accessed | tf_op | source)
XLA Modules:
  0.0 261.0 jit_solution(15489091943636024653)
XLA Ops:
  13.9 40.4 %all_to_all.52 = bf16[64,8,2048]{2,1,0:T(8,128)(2,1)} all-to-all(bf16[64,8,2048]{2,1,0:T(8,128)(2,1)S(1)} %fusion.23), channel_id=1, replica_groups=mesh['expert'=64,'tensor'=2] {'expert'}, dimensions={0} | all-to-all | bytes 4194304 | tf_op jit(solution)/shard_map/all_to_all | solution.py:86
  55.9 35.5 %all_to_all.53 = bf16[64,8,2048]{2,1,0:T(8,128)(2,1)} all-to-all(bf16[64,8,2048]{2,1,0:T(8,128)(2,1)S(1)} %fusion.22), channel_id=1, replica_groups=mesh['expert'=64,'tensor'=2] {'expert'}, dimensions={0} | all-to-all | bytes 4194304 | tf_op jit(solution)/shard_map/all_to_all | solution.py:43
  91.6 4.9 %fusion.8 = f32[512,384]{0,1:T(8,128)} fusion(bf16[64,8,4096]{2,1,0:T(8,128)(2,1)} %all-gather.6.cloned.1.call-done, bf16[1,384,4096]{2,1,0:T(8,128)(2,1)S(1)} %copy-done), kind=kOutput, calls=%fused_computation.15 | convolution fusion | flops 1610612736 | bytes 8126464 | tf_op jit(solution)/shard_map/dot_general | solution.py:14
  96.5 10.6 %all-gather.4.cloned.1.call-done = bf16[64,8,4096]{2,1,0:T(8,128)(2,1)} async-done(((bf16[64,8,2048]{2,1,0:T(8,128)(2,1)}), bf16[64,8,4096]{2,1,0:T(8,128)(2,1)}) %all-gather.4.cloned.1.call-update) | async-done | bytes 4194320 | tf_op jit(solution)/shard_map/all_gather | solution.py:50
  107.1 5.1 %fusion.12 = f32[512,384]{0,1:T(8,128)S(1)} fusion(bf16[64,8,4096]{2,1,0:T(8,128)(2,1)} %all-gather.4.cloned.1.call-done, bf16[1,384,4096]{2,1,0:T(8,128)(2,1)} %param.13), kind=kOutput, calls=%fused_computation.19 | convolution fusion | flops 1610612736 | bytes 8126464 | tf_op jit(solution)/shard_map/dot_general | solution.py:14
  112.5 2.9 %multiply_convert_fusion.1 = (bf16[512,384]{0,1:T(8,128)(2,1)S(1)}, bf16[512,384]{0,1:T(8,128)(2,1)S(1)}, bf16[512,384]{0,1:T(8,128)(2,1)}) fusion(f32[512,384]{0,1:T(8,128)S(1)} %copy-done.15, f32[512,384]{0,1:T(8,128)S(1)} %fusion.12, bf16[1,384,4096]{2,1,0:T(8,128)(2,1)S(1)} %copy-done.2, bf16[64,8,4096]{2,1,0:T(8,128)(2,1)S(1)} %copy-done.13), kind=kOutput, calls=%fused_computation.44 | convolution fusion | flops 1613561856 | bytes 10092544 | tf_op jit(solution)/shard_map/dot_general | solution.py:14
  117.5 5.3 %convolution_convert_fusion = bf16[512,4096]{1,0:T(8,128)(2,1)} fusion(bf16[512,384]{0,1:T(8,128)(2,1)} %get-tuple-element.17, bf16[1,384,4096]{2,1,0:T(8,128)(2,1)S(1)} %copy-done), kind=kOutput, calls=%fused_computation.7 | convolution fusion | flops 1612709888 | bytes 7733248 | tf_op jit(solution)/shard_map/dot_general | solution.py:58
  122.9 3.4 %copy.20 = bf16[1,384,4096]{1,2,0:T(8,128)(2,1)S(1)} copy(bf16[1,384,4096]{2,1,0:T(8,128)(2,1)} %param.12) | data formatting | bytes 6291456 | tf_op args[3]
  126.3 2.9 %copy.21 = bf16[384,2,2048]{2,0,1:T(8,128)(2,1)} copy(bf16[384,2,2048]{0,2,1:T(8,128)(2,1)S(1)} %bitcast.93) | data formatting | bytes 6291456 | tf_op jit(solution)/shard_map/all_to_all | solution.py:102
  129.2 5.7 %all-to-all-start.3 = ((bf16[384,2,2048]{2,0,1:T(8,128)(2,1)}), bf16[384,2,2048]{2,0,1:T(8,128)(2,1)}, u32[]{:S(2)}, u32[]{:S(2)}) async-start(bf16[384,2,2048]{2,0,1:T(8,128)(2,1)} %copy.21), calls=%async_computation.4 | async-start | bytes 6291456 | tf_op jit(solution)/shard_map/all_to_all | solution.py:102
  134.9 2.8 %copy.22 = bf16[1,384,4096]{1,2,0:T(8,128)(2,1)} copy(bf16[1,384,4096]{2,1,0:T(8,128)(2,1)S(1)} %copy-done.3) | data formatting | bytes 6291456 | tf_op args[4]
  137.6 3.2 %copy.23 = bf16[384,2,2048]{2,0,1:T(8,128)(2,1)S(1)} copy(bf16[384,2,2048]{0,2,1:T(8,128)(2,1)} %bitcast.94) | data formatting | bytes 6291456 | tf_op jit(solution)/shard_map/all_to_all | solution.py:103
  140.8 8.3 %all_to_all.54 = bf16[384,2,2048]{2,0,1:T(8,128)(2,1)} all-to-all(bf16[384,2,2048]{2,0,1:T(8,128)(2,1)S(1)} %copy.23), channel_id=1, replica_groups=mesh['expert'=64,'tensor'=2] {'tensor'}, dimensions={1} | all-to-all | bytes 6291456 | tf_op jit(solution)/shard_map/all_to_all | solution.py:103
  149.2 8.8 %bitcast_convert_fusion = bf16[2,512,2048]{2,1,0:T(8,128)(2,1)} fusion(bf16[512,2,2,384]{0,3,2,1:T(8,128)(2,1)} %bitcast.98, bf16[2,1,384,2048]{3,2,1,0:T(8,128)(2,1)} %bitcast.96, bf16[2,1,384,2048]{3,2,1,0:T(8,128)(2,1)} %bitcast.16), kind=kOutput, calls=%fused_computation.2 | convolution fusion | flops 3226468352 | bytes 12058624 | tf_op jit(solution)/shard_map/skcf,kcfd->ksd/dot_general | solution.py:115
  158.0 5.1 %reduce_sum.52 = bf16[512,2048]{1,0:T(8,128)(2,1)} reduce(bf16[2,512,2048]{2,1,0:T(8,128)(2,1)} %bitcast_convert_fusion, bf16[]{:T(256)} %constant.26.clone.1), dimensions={0}, to_apply=%region_5.7 | reduce | flops 1048576 | bytes 6291458 | tf_op jit(solution)/shard_map/reduce_sum | solution.py:122
  163.1 39.1 %all_to_all.55 = bf16[64,8,2048]{2,1,0:T(8,128)(2,1)S(1)} all-to-all(bf16[64,8,2048]{2,1,0:T(8,128)(2,1)} %bitcast.95), channel_id=1, replica_groups=mesh['expert'=64,'tensor'=2] {'expert'}, dimensions={0} | all-to-all | bytes 4194304 | tf_op jit(solution)/shard_map/all_to_all | solution.py:123
  202.2 7.3 %all-to-all-start.1 = ((bf16[64,8,2048]{2,1,0:T(8,128)(2,1)}), bf16[64,8,2048]{2,1,0:T(8,128)(2,1)}, u32[]{:S(2)}, u32[]{:S(2)}) async-start(bf16[64,8,2048]{2,1,0:T(8,128)(2,1)} %bitcast.97), calls=%async_computation.2 | async-start | bytes 4194304 | tf_op jit(solution)/shard_map/all_to_all | solution.py:62
  209.6 5.8 %fusion.6 = bf16[1,384,4096]{2,1,0:T(8,128)(2,1)} fusion(bf16[512,384]{0,1:T(8,128)(2,1)S(1)} %copy-done.8, bf16[64,8,4096]{2,1,0:T(8,128)(2,1)} %all-gather.6.cloned.1.call-done), kind=kOutput, calls=%fused_computation.13 | convolution fusion | flops 1612185600 | bytes 7733248 | tf_op jit(solution)/shard_map/dot_general | solution.py:8
  215.4 3.5 %fusion.4 = bf16[1,384,4096]{2,1,0:T(8,128)(2,1)} fusion(bf16[512,384]{0,1:T(8,128)(2,1)S(1)} %copy-done.7, bf16[64,8,4096]{2,1,0:T(8,128)(2,1)S(1)} %copy-done.14), kind=kOutput, calls=%fused_computation.11 | convolution fusion | flops 1612185600 | bytes 7733248 | tf_op jit(solution)/shard_map/dot_general | solution.py:8
  218.9 3.5 %fusion.5 = bf16[1,384,4096]{2,1,0:T(8,128)(2,1)} fusion(bf16[512,384]{0,1:T(8,128)(2,1)S(1)} %copy-done.5, bf16[64,8,4096]{2,1,0:T(8,128)(2,1)S(1)} %copy-done.14), kind=kOutput, calls=%fused_computation.12 | convolution fusion | flops 1612185600 | bytes 7733248 | tf_op jit(solution)/shard_map/dot_general | solution.py:8
  225.1 12.5 %all-to-all-done.1 = bf16[64,8,2048]{2,1,0:T(8,128)(2,1)} async-done(((bf16[64,8,2048]{2,1,0:T(8,128)(2,1)}), bf16[64,8,2048]{2,1,0:T(8,128)(2,1)}, u32[]{:S(2)}, u32[]{:S(2)}) %all-to-all-start.1) | async-done | bytes 2097184 | tf_op jit(solution)/shard_map/all_to_all | solution.py:62
  237.5 5.3 %gather_fusion = bf16[256,2048]{1,0:T(8,128)(2,1)} fusion(bf16[512,2048]{1,0:T(8,128)(2,1)} %bitcast.8, s32[1024]{0:T(1024)S(1)} %pad_clamp_fusion), kind=kCustom, calls=%fused_computation.clone | custom fusion | bytes 2098176 | tf_op jit(solution)/shard_map/jit(_take)/gather | solution.py:70
  244.5 3.5 %fusion.25 = bf16[32,2048]{1,0:T(8,128)(2,1)} fusion(f32[32,8]{1,0:T(8,128)S(1)} %copy.15, bf16[256,2048]{1,0:T(8,128)(2,1)} %gather_fusion, pred[256]{0:T(512)(128)(4,1)S(1)} %copy-done.12), kind=kLoop, calls=%fused_computation.35 | loop fusion | flops 2031616 | bytes 1180928 | tf_op jit(solution)/shard_map/reduce_sum | solution.py:74
  248.1 5.7 %psum.7 = f32[32,8]{1,0:T(8,128)S(1)} all-reduce(f32[32,8]{1,0:T(8,128)S(1)} %reduce_sum.55), channel_id=1, replica_groups=mesh['expert'=64,'tensor'=2] {'tensor'}, use_global_device_ids=true, to_apply=%region_8.10 | all-reduce | flops 256 | bytes 2048 | tf_op jit(solution)/shard_map/psum | solution.py:77
  (67 shorter events, 15.7 us)
Async XLA Ops:
  7.2 84.4 %copy-start = (bf16[1,384,4096]{2,1,0:T(8,128)(2,1)S(1)}, bf16[1,384,4096]{2,1,0:T(8,128)(2,1)}, u32[]{:S(2)}) copy-start(bf16[1,384,4096]{2,1,0:T(8,128)(2,1)} %param.14) | copy-start | bytes 9437188
  7.2 84.4 %all-gather.6.cloned.1.call-start = ((), (), s32[]{:S(2)}) async-start(), calls=%async_computation.9 | async-start | bytes 6291456 | tf_op jit(solution)/shard_map/all_gather | solution.py:93
  9.8 1.8 copy-start.10
  13.9 40.5 %copy-start.9 = (bf16[32,2048]{1,0:T(8,128)(2,1)S(1)}, bf16[32,2048]{1,0:T(8,128)(2,1)}, u32[]{:S(2)}) copy-start(bf16[32,2048]{1,0:T(8,128)(2,1)} %param.9) | copy-start | bytes 393220
  54.4 52.7 %all-gather.4.cloned.1.call-start = ((), (), s32[]{:S(2)}) async-start(), calls=%async_computation.7 | async-start | bytes 6291456 | tf_op jit(solution)/shard_map/all_gather | solution.py:50
  91.5 57.7 %all-gather.8.cloned.1.call-start = ((), (), s32[]{:S(2)}) async-start(), calls=%async_computation.10 | async-start | bytes 2359296 | tf_op jit(solution)/shard_map/all_gather | solution.py:113
  107.1 5.1 %copy-start.2 = (bf16[1,384,4096]{2,1,0:T(8,128)(2,1)S(1)}, bf16[1,384,4096]{2,1,0:T(8,128)(2,1)}, u32[]{:S(2)}) copy-start(bf16[1,384,4096]{2,1,0:T(8,128)(2,1)} %param.12) | copy-start | bytes 9437188
  107.1 5.3 %copy-start.13 = (bf16[64,8,4096]{2,1,0:T(8,128)(2,1)S(1)}, bf16[64,8,4096]{2,1,0:T(8,128)(2,1)}, u32[]{:S(2)}) copy-start(bf16[64,8,4096]{2,1,0:T(8,128)(2,1)} %all-gather.4.cloned.1.call-done) | copy-start | bytes 12582916
  107.1 5.4 %copy-start.15 = (f32[512,384]{0,1:T(8,128)S(1)}, f32[512,384]{0,1:T(8,128)}, u32[]{:S(2)}) copy-start(f32[512,384]{0,1:T(8,128)} %fusion.8) | copy-start | bytes 2359300
  115.5 0.7 copy-start.4
  115.5 0.9 copy-start.6
  117.3 84.9 %reduce-scatter.2.cloned.1.call-start = ((), (), s32[]{:S(2)}) async-start(), calls=%async_computation.8 | async-start | bytes 6291456 | tf_op jit(solution)/shard_map/reduce_scatter | solution.py:59
  129.2 5.7 %copy-start.3 = (bf16[1,384,4096]{2,1,0:T(8,128)(2,1)S(1)}, bf16[1,384,4096]{2,1,0:T(8,128)(2,1)}, u32[]{:S(2)}) copy-start(bf16[1,384,4096]{2,1,0:T(8,128)(2,1)} %param.13) | copy-start | bytes 9437188
  129.2 11.6 %all-to-all-start.3 = ((bf16[384,2,2048]{2,0,1:T(8,128)(2,1)}), bf16[384,2,2048]{2,0,1:T(8,128)(2,1)}, u32[]{:S(2)}, u32[]{:S(2)}) async-start(bf16[384,2,2048]{2,0,1:T(8,128)(2,1)} %copy.21), calls=%async_computation.4 | async-start | bytes 6291456 | tf_op jit(solution)/shard_map/all_to_all | solution.py:102
  202.2 7.3 %copy-start.11 = (s32[256]{0:T(256)S(1)}, s32[256]{0:T(256)}, u32[]{:S(2)}) copy-start(s32[256]{0:T(256)} %copy-done.10) | copy-start | bytes 3076
  202.2 7.4 %copy-start.8 = (bf16[512,384]{0,1:T(8,128)(2,1)S(1)}, bf16[512,384]{0,1:T(8,128)(2,1)}, u32[]{:S(2)}) copy-start(bf16[512,384]{0,1:T(8,128)(2,1)} %get-tuple-element.17) | copy-start | bytes 1179652
  202.2 35.3 %all-to-all-start.1 = ((bf16[64,8,2048]{2,1,0:T(8,128)(2,1)}), bf16[64,8,2048]{2,1,0:T(8,128)(2,1)}, u32[]{:S(2)}, u32[]{:S(2)}) async-start(bf16[64,8,2048]{2,1,0:T(8,128)(2,1)} %bitcast.97), calls=%async_computation.2 | async-start | bytes 4194304 | tf_op jit(solution)/shard_map/all_to_all | solution.py:62
  209.6 5.8 %copy-start.7 = (bf16[512,384]{0,1:T(8,128)(2,1)S(1)}, bf16[512,384]{0,1:T(8,128)(2,1)}, u32[]{:S(2)}) copy-start(bf16[512,384]{0,1:T(8,128)(2,1)} %copy-done.6) | copy-start | bytes 1179652
  209.6 5.8 %copy-start.14 = (bf16[64,8,4096]{2,1,0:T(8,128)(2,1)S(1)}, bf16[64,8,4096]{2,1,0:T(8,128)(2,1)}, u32[]{:S(2)}) copy-start(bf16[64,8,4096]{2,1,0:T(8,128)(2,1)} %all-gather.4.cloned.1.call-done) | copy-start | bytes 12582916
  215.4 3.6 %copy-start.5 = (bf16[512,384]{0,1:T(8,128)(2,1)S(1)}, bf16[512,384]{0,1:T(8,128)(2,1)}, u32[]{:S(2)}) copy-start(bf16[512,384]{0,1:T(8,128)(2,1)} %copy-done.4) | copy-start | bytes 1179652
  222.5 1.4 copy-start.12
  237.5 16.9 %copy-start.1 = (bf16[1,384,4096]{2,1,0:T(8,128)(2,1)S(1)}, bf16[1,384,4096]{2,1,0:T(8,128)(2,1)}, u32[]{:S(2)}) copy-start(bf16[1,384,4096]{2,1,0:T(8,128)(2,1)} %param.14) | copy-start | bytes 9437188
Sparse Core Ops, SparseCore 0:
  54.5 15.3 all-gather.5
  91.6 15.4 all-gather.3
  117.4 13.8 all-gather.7
  133.6 16.6 reduce-scatter.1
where the time goes:
time: 262 us; the launch traced here: 261 us
  blocking collectives  129 us (49%)
  matrix products  43.8 us (17%)
  waiting for transfers between devices  23.2 us (9%)
  local copies, waits for them, and re-layouts  23 us (9%)
  other arithmetic  14.5 us (6%)
  between operations  14 us (5%)
  starting transfers between devices  13.3 us (5%)
    all_to_all x1, blocking collectives, shards(): lax.all_to_all(send_grads.reshape(experts, capacity, local_width), 'exper...  40.4 us
    all_to_all x1, blocking collectives, shards(): lax.all_to_all(local_back.reshape(groups_count, capacity, local_width), '...  39.1 us
    all_to_all x1, blocking collectives, shards(): lax.all_to_all(send_rows.reshape(experts, capacity, local_width), 'expert...  35.5 us
    dot_general x4, matrix products, contract_rows(): lax.dot_general(left, right, (((0,), (0,)), ((), ())), preferred_element_...  14.4 us
    dot_general x3, matrix products, contract_cols(): lax.dot_general(left, right, (((1,), (1,)), ((), ())), preferred_element_...  12.9 us
    all_to_all x1, waiting for transfers between devices, shards(): lax.all_to_all(local_out.reshape(groups_count, capacity, local_width), 'e...  12.5 us
    all_gather x1, waiting for transfers between devices, shards(): lax.all_gather(received, 'tensor', axis=2, tiled=True)  10.6 us
    unnamed x37, local copies, waits for them, and re-layouts  9.76 us
  transfers between devices with their start and end apart: 6, of which 2 were waited for; matrix products, arithmetic and copies ran while one was open for 20% of the time, Pallas kernels for 0%

commit v1 on v0

v1 whole, which is shorter than its diff:
```python
import jax
import jax.numpy as jnp
from jax import lax
from jax.experimental import pallas as pl
from jax.experimental.pallas import tpu as pltpu
from jax.sharding import PartitionSpec as P

MESH = pl.DeviceIdType.MESH
BF = jnp.bfloat16
F32 = jnp.float32
ROUTES = ((0, 1, 2), (2, 0, 1), (1, 2, 0))
STRIDE = (16, 4, 1)
WIDE = (768, 768, 512)
FROM = (0, 768, 1536)
HALF = 2048
HID = 384
PARTS = range(3)


def nt(left, right):
    return lax.dot_general(left, right, (((1,), (1,)), ((), ())), preferred_element_type=F32)


def tn(left, right):
    return lax.dot_general(left, right, (((0,), (0,)), ((), ())), preferred_element_type=F32)


def nn(left, right):
    return jnp.dot(left, right, preferred_element_type=F32)


class Copies:
    def __init__(self, send_sems, recv_sems):
        self.send_sems, self.recv_sems, self.used, self.open = send_sems, recv_sems, 0, []

    def start(self, src, dst, device):
        copy = pltpu.make_async_remote_copy(
            src_ref=src,
            dst_ref=dst,
            send_sem=self.send_sems.at[self.used],
            recv_sem=self.recv_sems.at[self.used],
            device_id=device,
            device_id_type=MESH,
        )
        self.used += 1
        copy.start()
        self.open.append(copy)
        return copy

    def sent(self, copies):
        for copy in copies:
            copy.wait_send()
            self.open = [other for other in self.open if other is not copy]

    def finish(self):
        self.sent(list(self.open))


def main_kernel(*refs):
    refs = list(refs)

    def take(n):
        got = refs[:n]
        del refs[:n]
        return got

    tok, og, tab, gw, uw, dw = take(6)
    mixed, tgrad, rgo, t_out, g_out, h_out, gd_out, ud_out = take(8)
    ag = [take(3), take(3)]
    send = [take(3), take(3)]
    own = [take(3), take(3)]
    oth = [take(3), take(3)]
    tabs = take(3)
    pick = take(3)
    pickw = take(3)
    wcol = take(3)
    both = [take(3) for _ in range(3)]
    rest = [take(3) for _ in range(3)]
    part = take(3)
    gact, uact, fa, fb = take(4)
    hid = take(3)
    gdel = take(3)
    udel = take(3)
    qbuf, qsib, qrec, rgsend, rg2, rg1send, rg1 = take(7)
    crecv = [take(3), take(3)]
    prec = [take(3), take(3)]
    p1send = [take(3), take(3)]
    p1rec = [take(3), take(3)]
    send_sems, recv_sems, wsems, osems = take(4)

    me = lax.axis_index("expert")
    t = lax.axis_index("tensor")
    c = (me // 16, (me // 4) % 4, me % 4)
    remote = Copies(send_sems, recv_sems)
    sib = (me, 1 - t)

    def at(dim, j):
        return lax.rem(c[dim] + j, 4)

    def peer(dim, j):
        return (me + (at(dim, j) - c[dim]) * STRIDE[dim], t)

    def rows(i, n):
        return pl.ds(pl.multiple_of(i * n, n), n)

    loads = []
    for w, src in enumerate((gw, uw, dw)):
        for k in PARTS:
            mine = pl.ds(pl.multiple_of(t * HALF + FROM[k], 128), WIDE[k])
            other = pl.ds(pl.multiple_of((1 - t) * HALF + FROM[k], 128), WIDE[k])
            loads.append(pltpu.make_async_copy(src.at[0, :, mine], both[w][k].at[pl.ds(0, HID)], wsems.at[w * 6 + k * 2]))
            loads.append(pltpu.make_async_copy(src.at[0, :, other], rest[w][k], wsems.at[w * 6 + k * 2 + 1]))
    for load in loads:
        load.start()

    barrier = pltpu.get_barrier_semaphore()
    for dim in PARTS:
        for j in (1, 2, 3):
            pl.semaphore_signal(barrier, inc=1, device_id=peer(dim, j), device_id_type=MESH)
    pl.semaphore_signal(barrier, inc=1, device_id=sib, device_id_type=MESH)
    pl.semaphore_wait(barrier, 10)

    first = [[], []]
    first_tab = []
    for k in PARTS:
        d1, d2, _ = ROUTES[k]
        first_tab.append([remote.start(tab, tabs[k].at[c[d2], c[d1]], peer(d1, j)) for j in (2, 1, 3)])
    for s, src in enumerate((tok, og)):
        for k in PARTS:
            d1, d2, _ = ROUTES[k]
            cols = pl.ds(FROM[k], WIDE[k])
            here = rows(c[d2] * 4 + c[d1], 32)
            first[s].append([remote.start(src.at[:, cols], ag[s][k].at[here], peer(d1, j)) for j in (2, 1, 3)])
    for k in PARTS:
        d1, d2, _ = ROUTES[k]
        tabs[k][c[d2], c[d1]] = tab[...]
        for s, src in enumerate((tok, og)):
            ag[s][k][rows(c[d2] * 4 + c[d1], 32), :] = src[:, pl.ds(FROM[k], WIDE[k])]

    def second(s, k):
        for copy in first[s][k]:
            copy.wait_recv()
        d2 = ROUTES[k][1]
        block = ag[s][k].at[rows(c[d2], 128)]
        return [remote.start(block, block, peer(d2, j)) for j in (2, 1, 3)]

    second_tab, second_tok = [], []
    for k in PARTS:
        for copy in first_tab[k]:
            copy.wait_recv()
        d2 = ROUTES[k][1]
        second_tab.append([remote.start(tabs[k].at[c[d2]], tabs[k].at[c[d2]], peer(d2, j)) for j in (2, 1, 3)])
    for k in PARTS:
        second_tok.append(second(0, k))

    swaps = [[None] * 3 for _ in range(3)]
    for i, load in enumerate(loads):
        load.wait()
    for w in range(3):
        for k in PARTS:
            swaps[w][k] = remote.start(rest[w][k], both[w][k].at[pl.ds(HID, HID)], sib)

    lane = lax.broadcasted_iota(jnp.int32, (16, 128), 1) // 32
    tri_r = lax.broadcasted_iota(jnp.int32, (128, 128), 0)
    tri_c = lax.broadcasted_iota(jnp.int32, (128, 128), 1)
    before = jnp.where((tri_r // 32 == tri_c // 32) & (tri_r < tri_c), 1.0, 0.0).astype(BF)
    slot_row = lax.broadcasted_iota(jnp.int32, (128, 512), 0).astype(F32)
    block_base = (lax.broadcasted_iota(jnp.int32, (8, 512), 1) // 32 * 8).astype(F32)
    sub = lax.broadcasted_iota(jnp.int32, (8, 512), 0)
    table_ids = []
    for k in PARTS:
        d3 = ROUTES[k][2]
        for copy in second_tab[k]:
            copy.wait_recv()
        tiles = []
        for c2 in range(4):
            tile = tabs[k][c2, 0]
            for c1 in range(1, 4):
                tile = jnp.where(lane == c1, tabs[k][c2, c1], tile)
            tiles.append(tile)
        tile = jnp.concatenate(tiles, axis=1)
        ids, wts = tile[:8], tile[8:]
        if k == 0:
            table_ids = (ids, wts)
        hits = jnp.zeros((8, 512), F32)
        wds = []
        for d in range(4):
            expert = (me + (d - c[d3]) * STRIDE[d3]).astype(F32)
            same = ids == expert
            hits = jnp.where(sub == d, jnp.sum(jnp.where(same, 1.0, 0.0), axis=0, keepdims=True), hits)
            wds.append(jnp.sum(jnp.where(same, wts, 0.0), axis=0, keepdims=True))
        place = jnp.concatenate([nn(hits[:, i * 128 : i * 128 + 128].astype(BF), before) for i in range(4)], axis=1)
        key = jnp.where(hits > 0.0, place + block_base, -1.0)
        for d in range(4):
            hit = key[d : d + 1, :] == slot_row
            weight = jnp.where(hit, wds[d], 0.0)
            pick[k][pl.ds(d * 128, 128), :] = jnp.where(hit, 1.0, 0.0).astype(BF)
            pickw[k][pl.ds(d * 128, 128), :] = weight.astype(BF)
            wcol[k][pl.ds(d * 128, 128), :] = jnp.sum(weight, axis=1, keepdims=True)

    def third(s, k, copies):
        d3 = ROUTES[k][2]
        for copy in copies:
            copy.wait_recv()
        out = []
        for j in (2, 1, 3, 0):
            d = rows(at(d3, j), 128)
            got = nn(pick[k][d, :], ag[s][k][...])
            if s == 1:
                got = got * wcol[k][d, :]
            if j == 0:
                own[s][k][rows(c[d3], 128), :] = got.astype(BF)
            else:
                send[s][k][d, :] = got.astype(BF)
                out.append(remote.start(send[s][k].at[d], own[s][k].at[rows(c[d3], 128)], peer(d3, j)))
        return out

    def forward(s, k, copies):
        d3 = ROUTES[k][2]
        out = []
        for j, copy in zip((0, 1, 3, 2), (None, copies[1], copies[2], copies[0])):
            if copy is not None:
                copy.wait_recv()
            r = rows(at(d3, 4 - j), 128)
            out.append(remote.start(own[s][k].at[r], oth[s][k].at[r], sib))
        return out

    third_tok = [third(0, k, second_tok[k]) for k in PARTS]
    second_og = [second(1, k) for k in PARTS]
    cross_tok = [forward(0, k, third_tok[k]) for k in PARTS]
    third_og = [third(1, k, second_og[k]) for k in PARTS]

    keep = []

    def store(src, dst):
        copy = pltpu.make_async_copy(src, dst, osems.at[len(keep)])
        copy.start()
        keep.append(copy)

    def keep_rows(s, k, dst):
        mine = pl.ds(pl.multiple_of(t * HALF + FROM[k], 128), WIDE[k])
        other = pl.ds(pl.multiple_of((1 - t) * HALF + FROM[k], 128), WIDE[k])
        store(own[s][k], dst.at[:, mine])
        store(oth[s][k], dst.at[:, other])

    def spot(k, x, y, z):
        v = (z, y, x)
        d1, d2, d3 = ROUTES[k]
        return pl.ds(pl.multiple_of(((v[d3] * 4 + v[d2]) * 4 + v[d1]) * 8, 8), 8)

    def contract(s, w, k):
        part[k][...] = nt(own[s][k][...], both[w][k][pl.ds(0, HID), :]) + nt(oth[s][k][...], rest[w][k][...])

    def gather_parts(dst):
        def body(i, carry):
            y, z = i // 4, i % 4
            for x in range(4):
                dst[spot(0, x, y, z), :] = (
                    part[0][spot(0, x, y, z), :] + part[1][spot(1, x, y, z), :] + part[2][spot(2, x, y, z), :]
                )
            return carry

        lax.fori_loop(0, 16, body, 0)

    def spread(src, dst):
        dst[0][:, pl.ds(0, HID)] = src[...].astype(BF)

        def body(i, carry):
            a, b = i // 4, i % 4
            group = rows(i, 32)
            dst[1][group, pl.ds(0, HID)] = jnp.concatenate([src[spot(0, x, a, b), :] for x in range(4)], axis=0).astype(BF)
            dst[2][group, pl.ds(0, HID)] = jnp.concatenate([src[spot(0, b, y, a), :] for y in range(4)], axis=0).astype(BF)
            return carry

        lax.fori_loop(0, 16, body, 0)

    def swap_cols(dst):
        return [remote.start(dst[k].at[:, pl.ds(0, HID)], dst[k].at[:, pl.ds(HID, HID)], sib) for k in PARTS]

    for k in PARTS:
        for copy in cross_tok[k]:
            copy.wait_recv()
        keep_rows(0, k, t_out)
    for k in PARTS:
        contract(0, 0, k)
    gather_parts(gact)
    for k in PARTS:
        contract(0, 1, k)
    gather_parts(uact)
    gate = gact[...]
    fa[...] = gate * jax.nn.sigmoid(gate) * uact[...]
    spread(fa, hid)
    cross_hid = swap_cols(hid)
    for k in PARTS:
        store(hid[k].at[:, pl.ds(0, HID)], h_out.at[k])

    cross_og = [forward(1, k, third_og[k]) for k in PARTS]

    def back3(s, k):
        d3 = ROUTES[k][2]
        out = []
        for j in (2, 1, 3):
            out.append(remote.start(send[s][k].at[rows(at(d3, j), 128)], crecv[s][k].at[rows(c[d3], 128)], peer(d3, j)))
        crecv[s][k][rows(c[d3], 128), :] = send[s][k][rows(c[d3], 128), :]
        return out

    def back2(s, k, copies):
        for copy in copies:
            copy.wait_recv()
        ag[s][k][...] = tn((pickw, pick)[s][k][...], crecv[s][k][...]).astype(BF)
        d2 = ROUTES[k][1]
        return [remote.start(ag[s][k].at[rows(at(d2, j), 128)], prec[s][k].at[j - 1], peer(d2, j)) for j in (2, 1, 3)]

    def back1(s, k, copies):
        for copy in copies:
            copy.wait_recv()
        d1, d2, _ = ROUTES[k]
        total = ag[s][k][rows(c[d2], 128), :].astype(F32)
        for j in range(3):
            total = total + prec[s][k][j].astype(F32)
        p1send[s][k][...] = total.astype(BF)
        return [remote.start(p1send[s][k].at[rows(at(d1, j), 32)], p1rec[s][k].at[j - 1], peer(d1, j)) for j in (2, 1, 3)]

    def back0(s, k, copies, dst):
        for copy in copies:
            copy.wait_recv()
        total = p1send[s][k][rows(c[ROUTES[k][0]], 32), :].astype(F32)
        for j in range(3):
            total = total + p1rec[s][k][j].astype(F32)
        dst[:, pl.ds(FROM[k], WIDE[k])] = total.astype(BF)

    out3 = []
    for k in PARTS:
        swaps[2][k].wait_recv()
        cross_hid[k].wait_recv()
        remote.sent(second_tok[k])
        remote.sent(third_tok[k])
        send[0][k][...] = nn(hid[k][...], both[2][k][...]).astype(BF)
        out3.append(back3(0, k))

    for k in PARTS:
        for copy in cross_og[k]:
            copy.wait_recv()
        keep_rows(1, k, g_out)
    for k in PARTS:
        contract(1, 2, k)
    gather_parts(fb)
    qprod = fa[...].astype(BF).astype(F32) * fb[...]
    qbuf[...] = lax.dot_general(
        jnp.ones((8, HID), F32), qprod, (((1,), (1,)), ((), ())), precision=lax.Precision.HIGHEST, preferred_element_type=F32
    )
    cross_q = remote.start(qbuf, qsib, sib)
    gate = gact[...]
    sg = jax.nn.sigmoid(gate)
    fa[...] = fb[...] * uact[...] * sg * (1.0 + gate * (1.0 - sg))
    spread(fa, gdel)
    cross_gd = swap_cols(gdel)
    fa[...] = fb[...] * (gate * sg)
    spread(fa, udel)
    cross_ud = swap_cols(udel)
    for k in PARTS:
        store(gdel[k].at[:, pl.ds(0, HID)], gd_out.at[k])
        store(udel[k].at[:, pl.ds(0, HID)], ud_out.at[k])

    out2 = [back2(0, k, out3[k]) for k in PARTS]

    d1, d2, d3 = ROUTES[0]
    cross_q.wait_recv()
    q = qbuf[...] + qsib[...]
    for i in range(4):
        rgsend[i] = q[:, i * 128 : i * 128 + 128]
    rg3 = [remote.start(rgsend.at[at(d3, j)], qrec.at[c[d3]], peer(d3, j)) for j in (2, 1, 3)]
    qrec[c[d3]] = rgsend[c[d3]]

    bk3 = []
    for k in PARTS:
        for w in range(2):
            swaps[w][k].wait_recv()
        cross_gd[k].wait_recv()
        cross_ud[k].wait_recv()
        remote.sent(second_og[k])
        remote.sent(third_og[k])
        send[1][k][...] = (nn(gdel[k][...], both[0][k][...]) + nn(udel[k][...], both[1][k][...])).astype(BF)
        bk3.append(back3(1, k))

    for copy in rg3:
        copy.wait_recv()
    ids, wts = table_ids
    rg = jnp.zeros((8, 512), F32)
    for d in range(4):
        value = jnp.dot(
            qrec[d],
            pick[0][pl.ds(d * 128, 128), :].astype(F32),
            precision=lax.Precision.HIGHEST,
            preferred_element_type=F32,
        )
        expert = (me + (d - c[d3]) * STRIDE[d3]).astype(F32)
        rg = rg + jnp.where(ids == expert, value, 0.0)
    rg = rg / wts
    remote.sent(rg3)
    for i in range(4):
        rgsend[i] = rg[:, i * 128 : i * 128 + 128]
    rgc2 = [remote.start(rgsend.at[at(d2, j)], rg2.at[j - 1], peer(d2, j)) for j in (2, 1, 3)]

    out1 = [back1(0, k, out2[k]) for k in PARTS]
    for copy in rgc2:
        copy.wait_recv()
    rg1send[...] = rgsend[c[d2]] + rg2[0] + rg2[1] + rg2[2]
    rgc1 = [remote.start(rg1send, rg1.at[j - 1], peer(d1, j)) for j in (2, 1, 3)]
    bk2 = [back2(1, k, bk3[k]) for k in PARTS]
    for k in PARTS:
        back0(0, k, out1[k], mixed)
    for copy in rgc1:
        copy.wait_recv()
    rgo[...] = rg1send[...] + rg1[0] + rg1[1] + rg1[2]
    bk1 = [back1(1, k, bk2[k]) for k in PARTS]
    for copy in keep:
        copy.wait()
    for k in PARTS:
        back0(1, k, bk1[k], tgrad)
    remote.finish()


N_COPIES = 220


def run_main(tok, og, tab, gw, uw, dw):
    vm = pltpu.VMEM
    scratch = []

    def per(make):
        scratch.extend(make(WIDE[k]) for k in PARTS)

    for _ in range(8):
        per(lambda w: vm((512, w), BF))
    per(lambda w: vm((4, 4, 16, 128), F32))
    per(lambda w: vm((512, 512), BF))
    per(lambda w: vm((512, 512), BF))
    per(lambda w: vm((512, 1), F32))
    for _ in range(3):
        per(lambda w: vm((2 * HID, w), BF))
    for _ in range(3):
        per(lambda w: vm((HID, w), BF))
    per(lambda w: vm((512, HID), F32))
    scratch.extend(vm((512, HID), F32) for _ in range(4))
    for _ in range(3):
        per(lambda w: vm((512, 2 * HID), BF))
    scratch.extend(vm(s, F32) for s in ((8, 512), (8, 512), (4, 8, 128), (4, 8, 128), (3, 8, 128), (8, 128), (3, 8, 128)))
    for _ in range(2):
        per(lambda w: vm((512, w), BF))
    for _ in range(2):
        per(lambda w: vm((3, 128, w), BF))
    for _ in range(2):
        per(lambda w: vm((128, w), BF))
    for _ in range(2):
        per(lambda w: vm((3, 32, w), BF))
    scratch.extend(
        [
            pltpu.SemaphoreType.DMA((N_COPIES,)),
            pltpu.SemaphoreType.DMA((N_COPIES,)),
            pltpu.SemaphoreType.DMA((18,)),
            pltpu.SemaphoreType.DMA((24,)),
        ]
    )
    in_vmem = pl.BlockSpec(memory_space=pltpu.VMEM)
    anywhere = pl.BlockSpec(memory_space=pl.ANY)
    shape = jax.ShapeDtypeStruct
    return pl.pallas_call(
        main_kernel,
        out_shape=(
            shape((32, HALF), BF),
            shape((32, HALF), BF),
            shape((8, 128), F32),
            shape((512, 2 * HALF), BF),
            shape((512, 2 * HALF), BF),
            shape((3, 512, HID), BF),
            shape((3, 512, HID), BF),
            shape((3, 512, HID), BF),
        ),
        in_specs=[in_vmem] * 3 + [anywhere] * 3,
        out_specs=(in_vmem,) * 3 + (anywhere,) * 5,
        scratch_shapes=scratch,
        compiler_params=pltpu.CompilerParams(collective_id=0, has_side_effects=True, vmem_limit_bytes=63 * 2**20),
        cost_estimate=pl.CostEstimate(flops=10**10, bytes_accessed=2 * 10**7, transcendentals=10**6),
    )(tok, og, tab, gw, uw, dw)


def grads_kernel(t_ref, g_ref, h_ref, gd_ref, ud_ref, gg_ref, ug_ref, dg_ref):
    gg_ref[0] = tn(gd_ref[0], t_ref[...]).astype(BF)
    ug_ref[0] = tn(ud_ref[0], t_ref[...]).astype(BF)
    dg_ref[0] = tn(h_ref[0], g_ref[...]).astype(BF)


def run_grads(t_rows, g_rows, h, gd, ud):
    tile = 256
    cols = pl.BlockSpec((512, tile), lambda i: (0, i))
    left = pl.BlockSpec((1, 512, HID), lambda i: (i % 8 // 3, 0, 0))
    out = pl.BlockSpec((1, HID, tile), lambda i: (0, 0, i))
    return pl.pallas_call(
        grads_kernel,
        grid=(2 * HALF // tile,),
        out_shape=(jax.ShapeDtypeStruct((1, HID, 2 * HALF), BF),) * 3,
        in_specs=[cols, cols, left, left, left],
        out_specs=(out,) * 3,
        compiler_params=pltpu.CompilerParams(vmem_limit_bytes=48 * 2**20),
        cost_estimate=pl.CostEstimate(flops=5 * 10**9, bytes_accessed=2 * 10**7, transcendentals=0),
    )(t_rows, g_rows, h, gd, ud)


def shards(tokens, route_ids, route_weight, gate_weight, up_weight, down_weight, out_grad):
    tab = jnp.concatenate(
        [jnp.tile(route_ids.astype(F32).T, (1, 4)), jnp.tile(route_weight.T, (1, 4))], axis=0
    )
    mixed, tgrad, rg, t_rows, g_rows, h, gd, ud = run_main(
        tokens, out_grad, tab, gate_weight, up_weight, down_weight
    )
    gate_grad, up_grad, down_grad = run_grads(t_rows, g_rows, h, gd, ud)
    z = lax.axis_index("expert") // 16
    route_grad = lax.dynamic_slice_in_dim(rg, z * 32, 32, axis=1).T
    return (mixed, tgrad, route_grad, gate_grad, up_grad, down_grad)


def solution(mesh):
    placed = (
        P("expert", "tensor"),
        P("expert", None),
        P("expert", None),
        P("expert", "tensor", None),
        P("expert", "tensor", None),
        P("expert", "tensor", None),
        P("expert", "tensor"),
    )
    return jax.shard_map(
        shards,
        mesh=mesh,
        in_specs=placed,
        out_specs=(
            P("expert", "tensor"),
            P("expert", "tensor"),
            P("expert", None),
            P("expert", "tensor", None),
            P("expert", "tensor", None),
            P("expert", "tensor", None),
        ),
        check_vma=False,
    )
```

time: 262 us -> 134 us (0.51)
  blocking collectives: 129 us -> 0 us
  Pallas kernels: 0 us -> 124 us
  matrix products: 43.8 us -> 0 us
  waiting for transfers between devices: 23.2 us -> 0 us
  local copies, waits for them, and re-layouts: 23 us -> 7.34 us
  between operations: 14 us -> 0.67 us
  starting transfers between devices: 13.3 us -> 0 us
  other arithmetic: 14.5 us -> 1.29 us
    pallas_call x0 -> x2, Pallas kernels: none -> 124 us  [the longest x1 109 us: run_main(): pl.pallas_call(main_kernel, out_shape=(shape((32, HALF), BF), shape((32,...]
    all_to_all x4 -> x0, blocking collectives: 123 us -> none  [the longest x1 40.4 us: shards(): lax.all_to_all(send_grads.reshape(experts, capacity, local_width), 'exper...]
    dot_general x10 -> x0, matrix products: 43.8 us -> none  [the longest x4 14.4 us: contract_rows(): lax.dot_general(left, right, (((0,), (0,)), ((), ())), preferred_element_...]
    all_to_all x2 -> x0, starting transfers between devices: 13 us -> none  [the longest x1 7.32 us: shards(): lax.all_to_all(local_out.reshape(groups_count, capacity, local_width), 'e...]
    all_to_all x2 -> x0, waiting for transfers between devices: 12.5 us -> none  [the longest x1 12.5 us: shards(): lax.all_to_all(local_out.reshape(groups_count, capacity, local_width), 'e...]
    reduce_sum x5 -> x0, other arithmetic: 11.5 us -> none  [the longest x1 5.08 us: shards(): local_back = jnp.sum(rounded, axis=0).astype(jnp.bfloat16)]
    all_gather x3 -> x0, waiting for transfers between devices: 10.6 us -> none  [the longest x1 10.6 us: shards(): lax.all_gather(received, 'tensor', axis=2, tiled=True)]
    gather x2 -> x0, local copies, waits for them, and re-layouts: 6.69 us -> none  [the longest x1 5.34 us: shards(): jnp.take(returned.reshape(experts * capacity, local_width), slot_index, a...]
  transfers between devices with their start and end apart: 6 -> 0, of which waited for: 2 -> 0; matrix products, arithmetic and copies ran while one was open for 20% -> 0% of each run, Pallas kernels for 0% -> 0%
where the time goes in v1:
time: 134 us
  Pallas kernels  124 us (93%)
  local copies, waits for them, and re-layouts  7.34 us (5%)
    pallas_call x1, Pallas kernels, run_main(): pl.pallas_call(main_kernel, out_shape=(shape((32, HALF), BF), shape((32,...  109 us
    pallas_call x1, Pallas kernels, run_grads(): pl.pallas_call(grads_kernel, grid=(2 * HALF // tile,), out_shape=(jax.Sha...  15.1 us
    unnamed x12, local copies, waits for them, and re-layouts  5.13 us

profile of v1, /device:TPU:1, one launch (start us, length us, event | category | flops | bytes accessed | tf_op | source)
XLA Modules:
  0.0 133.6 jit_solution(8284786176685420146)
XLA Ops:
  0.7 0.7 convert_bitcast_fusion
  1.3 0.1 tile.9
  1.4 0.7 tile.20
  2.1 0.1 tile.21
  2.2 0.6 pad_maximum_fusion.refs_2_
  2.8 109.2 %shard_map.118 = (bf16[32,2048]{1,0:T(8,128)(2,1)}, bf16[32,2048]{1,0:T(8,128)(2,1)}, f32[8,128]{1,0:T(8,128)}, bf16[512,4096]{1,0:T(8,128)(2,1)}, bf16[512,4096...) custom-call(bf16[32,2048]{1,0:T(8,128)(2,1)} %refs_0_.1, ...), custom_call_target="tpu_custom_call" | custom-call | flops 10000000000 | bytes 20000000 | tf_op jit(solution)/shard_map/pallas_call | solution.py:468
  112.0 1.4 %dynamic-slice_bitcast_fusion = f32[32,8]{0,1:T(8,128)} fusion(f32[8,128]{1,0:T(8,128)} %get-tuple-element.19, s32[]{:T(128)S(6)} %select_n.9), kind=kLoop, calls=%fused_computation.1 | loop fusion | bytes 2052 | tf_op jit(solution)/shard_map/transpose | solution.py:519
  113.4 0.0 copy-start
  113.4 1.3 copy-done
  114.7 0.0 copy-start.1
  114.7 1.3 copy-done.1
  115.9 0.0 copy-start.2
  115.9 1.3 copy-done.2
  117.2 0.0 copy-start.4
  117.2 0.0 copy-start.3
  117.2 15.1 %shard_map.119 = (bf16[1,384,4096]{2,1,0:T(8,128)(2,1)}, bf16[1,384,4096]{2,1,0:T(8,128)(2,1)}, bf16[1,384,4096]{2,1,0:T(8,128)(2,1)}) custom-call(bf16[512,4096]{1,0:T(8,128)(2,1)} %get-tuple-element.20.t_ref, bf16[512,4096]{1,0:T(8,128)(2,1)} %get-tuple-element.21.g_ref, bf16[3,512,384]{2,1,0:T(8,128)(2,1)S(1)} %copy-done, ...), custom_call_target="tpu_custom_call" | custom-call | flops 5000000000 | bytes 20000000 | tf_op jit(solution)/shard_map/pallas_call | solution.py:499
  132.3 0.0 copy-done.4
  132.3 0.7 copy.15
  132.9 0.0 copy-done.3
  132.9 0.7 copy.16
  (1 shorter events, 0.0 us)
Async XLA Ops:
  113.4 1.3 copy-start
  114.7 1.3 copy-start.1
  115.9 1.3 copy-start.2
  117.2 15.1 %copy-start.4 = (bf16[32,2048]{1,0:T(8,128)(2,1)S(1)}, bf16[32,2048]{1,0:T(8,128)(2,1)}, u32[]{:S(2)}) copy-start(bf16[32,2048]{1,0:T(8,128)(2,1)} %get-tuple-element.34) | copy-start | bytes 393220
  117.2 15.7 %copy-start.3 = (bf16[32,2048]{1,0:T(8,128)(2,1)S(1)}, bf16[32,2048]{1,0:T(8,128)(2,1)}, u32[]{:S(2)}) copy-start(bf16[32,2048]{1,0:T(8,128)(2,1)} %get-tuple-element.35) | copy-start | bytes 393220

commit v2 on v1

v2 whole, which is shorter than its diff:
```python
import jax
import jax.numpy as jnp
from jax import lax
from jax.experimental import pallas as pl
from jax.experimental.pallas import tpu as pltpu
from jax.sharding import PartitionSpec as P

MESH = pl.DeviceIdType.MESH
BF = jnp.bfloat16
F32 = jnp.float32
ROUTES = ((0, 1, 2), (2, 0, 1), (1, 2, 0))
STRIDE = (16, 4, 1)
WIDE = (768, 768, 512)
FROM = (0, 768, 1536)
HALF = 2048
HID = 384
PARTS = range(3)


def nt(left, right):
    return lax.dot_general(left, right, (((1,), (1,)), ((), ())), preferred_element_type=F32)


def tn(left, right):
    return lax.dot_general(left, right, (((0,), (0,)), ((), ())), preferred_element_type=F32)


def nn(left, right):
    return jnp.dot(left, right, preferred_element_type=F32)


class Group:
    def __init__(self, index, send_sem, recv_sem, whole, device):
        self.index, self.send_sem, self.recv_sem, self.open = index, send_sem, recv_sem, True
        self.all = pltpu.make_async_remote_copy(
            src_ref=whole, dst_ref=whole, send_sem=send_sem, recv_sem=recv_sem, device_id=device, device_id_type=MESH
        )

    def start(self, src, dst, device):
        pltpu.make_async_remote_copy(
            src_ref=src, dst_ref=dst, send_sem=self.send_sem, recv_sem=self.recv_sem, device_id=device, device_id_type=MESH
        ).start()

    def arrived(self):
        self.all.wait_recv()

    def sent(self):
        if self.open:
            self.all.wait_send()
        self.open = False


class Copies:
    def __init__(self, send_sems, recv_sems, device):
        self.send_sems, self.recv_sems, self.device, self.groups = send_sems, recv_sems, device, []

    def group(self, whole):
        i = len(self.groups)
        self.groups.append(Group(i, self.send_sems.at[i], self.recv_sems.at[i], whole, self.device))
        return self.groups[i]

    def one(self, src, dst, device):
        group = self.group(src)
        group.start(src, dst, device)
        return group

    def finish(self):
        for group in self.groups:
            group.sent()


def main_kernel(*refs):
    refs = list(refs)

    def take(n):
        got = refs[:n]
        del refs[:n]
        return got

    tok, og, ids_in, wts_in, gw, uw, dw = take(7)
    mixed, tgrad, rgo, t_out, g_out, h_out, gd_out, ud_out = take(8)
    (tab,) = take(1)
    ag = [take(3), take(3)]
    send = [take(3), take(3)]
    own = [take(3), take(3)]
    oth = [take(3), take(3)]
    tabs = take(3)
    pick = take(3)
    pickw = take(3)
    wcol = take(3)
    both = [take(3) for _ in range(3)]
    rest = [take(3) for _ in range(3)]
    part = take(3)
    gact, uact, fa, fb = take(4)
    hid = take(3)
    gdel = take(3)
    udel = take(3)
    qbuf, qsib, qrec, rgsend, rg2, rg1send, rg1 = take(7)
    crecv = [take(3), take(3)]
    prec = [take(3), take(3)]
    p1send = [take(3), take(3)]
    p1rec = [take(3), take(3)]
    send_sems, recv_sems, wsems, osems = take(4)

    me = lax.axis_index("expert")
    t = lax.axis_index("tensor")
    c = (me // 16, (me // 4) % 4, me % 4)
    sib = (me, 1 - t)
    remote = Copies(send_sems, recv_sems, sib)

    def at(dim, j):
        return lax.rem(c[dim] + j, 4)

    def peer(dim, j):
        return (me + (at(dim, j) - c[dim]) * STRIDE[dim], t)

    def rows(i, n):
        return pl.ds(pl.multiple_of(i * n, n), n)

    def expert_at(d3, d):
        return (me + (d - c[d3]) * STRIDE[d3]).astype(F32)

    barrier = pltpu.get_barrier_semaphore()
    for dim in PARTS:
        for j in (1, 2, 3):
            pl.semaphore_signal(barrier, inc=1, device_id=peer(dim, j), device_id_type=MESH)
    pl.semaphore_signal(barrier, inc=1, device_id=sib, device_id_type=MESH)

    loads = []
    for w, src in enumerate((gw, uw, dw)):
        for k in PARTS:
            mine = pl.ds(pl.multiple_of(t * HALF + FROM[k], 128), WIDE[k])
            other = pl.ds(pl.multiple_of((1 - t) * HALF + FROM[k], 128), WIDE[k])
            pltpu.make_async_copy(src.at[0, :, other], rest[w][k], wsems.at[w]).start()
            pltpu.make_async_copy(src.at[0, :, mine], both[w][k].at[pl.ds(0, HID)], wsems.at[w]).start()
        loads.append(pltpu.make_async_copy(src, src, wsems.at[w]))

    tab[0:8, :] = jnp.concatenate([ids_in[...].astype(F32)] * 4, axis=1)
    tab[8:16, :] = jnp.concatenate([wts_in[...]] * 4, axis=1)
    for k in PARTS:
        d1, d2, _ = ROUTES[k]
        tabs[k][c[d2], c[d1]] = tab[...]
        for s, src in enumerate((tok, og)):
            ag[s][k][rows(c[d2] * 4 + c[d1], 32), :] = src[:, pl.ds(FROM[k], WIDE[k])]
    pl.semaphore_wait(barrier, 10)

    first = [[], []]
    first_tab = []
    for k in PARTS:
        d1, d2, _ = ROUTES[k]
        first_tab.append(remote.group(tabs[k].at[0, pl.ds(0, 3)]))
        for j in (2, 1, 3):
            first_tab[k].start(tab, tabs[k].at[c[d2], c[d1]], peer(d1, j))
    for s, src in enumerate((tok, og)):
        for k in PARTS:
            d1, d2, _ = ROUTES[k]
            cols = pl.ds(FROM[k], WIDE[k])
            here = rows(c[d2] * 4 + c[d1], 32)
            first[s].append(remote.group(ag[s][k].at[pl.ds(0, 96)]))
            for j in (2, 1, 3):
                first[s][k].start(src.at[:, cols], ag[s][k].at[here], peer(d1, j))

    def second(s, k):
        first[s][k].arrived()
        d2 = ROUTES[k][1]
        block = ag[s][k].at[rows(c[d2], 128)]
        return {j: remote.one(block, block, peer(d2, j)) for j in (2, 1, 3)}

    lane16 = lax.broadcasted_iota(jnp.int32, (16, 128), 1) // 32
    tri_r = lax.broadcasted_iota(jnp.int32, (128, 128), 0)
    tri_c = lax.broadcasted_iota(jnp.int32, (128, 128), 1)
    before = jnp.where((tri_r // 32 == tri_c // 32) & (tri_r < tri_c), 1.0, 0.0).astype(BF)
    slot_row = lax.broadcasted_iota(jnp.int32, (32, 128), 0).astype(F32)
    lane8 = lax.broadcasted_iota(jnp.int32, (8, 128), 1) // 32
    block_base = (lane8 * 8).astype(F32)
    sub8 = lax.broadcasted_iota(jnp.int32, (8, 128), 0)

    def table(k, c2):
        tile = tabs[k][c2, 0]
        for c1 in range(1, 4):
            tile = jnp.where(lane16 == c1, tabs[k][c2, c1], tile)
        return tile[:8], tile[8:]

    def tables(k, c2):
        d3 = ROUTES[k][2]
        ids, wts = table(k, c2)
        hits = jnp.zeros((8, 128), F32)
        wds = []
        for d in range(4):
            same = ids == expert_at(d3, d)
            hits = jnp.where(sub8 == d, jnp.sum(jnp.where(same, 1.0, 0.0), axis=0, keepdims=True), hits)
            wds.append(jnp.sum(jnp.where(same, wts, 0.0), axis=0, keepdims=True))
        key = jnp.where(hits > 0.0, nn(hits.astype(BF), before) + block_base, -1.0)
        hit = [key[d : d + 1, :] == slot_row for d in range(4)]
        weight = jnp.concatenate([jnp.where(hit[d], wds[d], 0.0) for d in range(4)], axis=0)
        group = rows(c2, 128)
        pick[k][group, :] = jnp.concatenate([jnp.where(h, 1.0, 0.0) for h in hit], axis=0).astype(BF)
        pickw[k][group, :] = weight.astype(BF)
        wcol[k][group, :] = jnp.sum(weight, axis=1, keepdims=True)

    def third(s, k, j):
        _, d2, d3 = ROUTES[k]
        c2 = at(d2, j)
        group = rows(c2, 128)
        got = nn(pick[k][group, :], ag[s][k][group, :])
        if s == 1:
            got = got * wcol[k][group, :]
        send[s][k][group, :] = got.astype(BF)
        here = rows(c[d3] * 4 + c2, 32)
        for j3 in (2, 1, 3):
            thirds[s][k][j3].start(send[s][k].at[rows(c2 * 4 + at(d3, j3), 32)], own[s][k].at[here], peer(d3, j3))
        own[s][k][here, :] = send[s][k][rows(c2 * 4 + c[d3], 32), :]

    def forward(s, k):
        d3 = ROUTES[k][2]
        out = remote.group(oth[s][k])
        for j3 in (0, 1, 3, 2):
            if j3:
                thirds[s][k][j3].arrived()
            r = rows(at(d3, 4 - j3), 128)
            out.start(own[s][k].at[r], oth[s][k].at[r], sib)
        return out

    thirds = [[{j3: remote.group(own[s][k].at[pl.ds(0, 128)]) for j3 in (1, 2, 3)} for k in PARTS] for s in range(2)]
    seconds, second_tab = [[], []], []
    for k in PARTS:
        first_tab[k].arrived()
        d2 = ROUTES[k][1]
        second_tab.append({j: remote.one(tabs[k].at[c[d2]], tabs[k].at[c[d2]], peer(d2, j)) for j in (2, 1, 3)})
    for k in PARTS:
        seconds[0].append(second(0, k))
    for k in PARTS:
        tables(k, c[ROUTES[k][1]])
        third(0, k, 0)
    for k in PARTS:
        seconds[1].append(second(1, k))
    for k in PARTS:
        third(1, k, 0)

    for load in loads:
        load.wait()
    swaps = [[remote.one(rest[w][k], both[w][k].at[pl.ds(HID, HID)], sib) for k in PARTS] for w in range(3)]

    for j in (1, 3, 2):
        for k in PARTS:
            second_tab[k][j].arrived()
            tables(k, at(ROUTES[k][1], 4 - j))
            seconds[0][k][j].arrived()
            third(0, k, 4 - j)
    for j in (1, 3, 2):
        for k in PARTS:
            seconds[1][k][j].arrived()
            third(1, k, 4 - j)

    def store(src, dst, i):
        pltpu.make_async_copy(src, dst, osems.at[i]).start()

    def keep_rows(s, k, dst):
        mine = pl.ds(pl.multiple_of(t * HALF + FROM[k], 128), WIDE[k])
        other = pl.ds(pl.multiple_of((1 - t) * HALF + FROM[k], 128), WIDE[k])
        store(own[s][k], dst.at[:, mine], s)
        store(oth[s][k], dst.at[:, other], s)

    def spot(k, x, y, z):
        v = (z, y, x)
        d1, d2, d3 = ROUTES[k]
        return pl.ds(pl.multiple_of(((v[d3] * 4 + v[d2]) * 4 + v[d1]) * 8, 8), 8)

    def contract(s, w, k):
        part[k][...] = nt(own[s][k][...], both[w][k][pl.ds(0, HID), :]) + nt(oth[s][k][...], rest[w][k][...])

    def gather_parts(dst):
        def body(i, carry):
            y, z = i // 4, i % 4
            for x in range(4):
                dst[spot(0, x, y, z), :] = (
                    part[0][spot(0, x, y, z), :] + part[1][spot(1, x, y, z), :] + part[2][spot(2, x, y, z), :]
                )
            return carry

        lax.fori_loop(0, 16, body, 0)

    def spread(src, dst):
        dst[0][:, pl.ds(0, HID)] = src[...].astype(BF)

        def body(i, carry):
            a, b = i // 4, i % 4
            group = rows(i, 32)
            dst[1][group, pl.ds(0, HID)] = jnp.concatenate([src[spot(0, x, a, b), :] for x in range(4)], axis=0).astype(BF)
            dst[2][group, pl.ds(0, HID)] = jnp.concatenate([src[spot(0, b, y, a), :] for y in range(4)], axis=0).astype(BF)
            return carry

        lax.fori_loop(0, 16, body, 0)

    def swap_cols(dst):
        return [remote.one(dst[k].at[:, pl.ds(0, HID)], dst[k].at[:, pl.ds(HID, HID)], sib) for k in PARTS]

    cross_tok = [forward(0, k) for k in PARTS]
    for k in PARTS:
        cross_tok[k].arrived()
        keep_rows(0, k, t_out)
        contract(0, 0, k)
    gather_parts(gact)
    for k in PARTS:
        contract(0, 1, k)
    gather_parts(uact)
    gate = gact[...]
    fa[...] = gate * jax.nn.sigmoid(gate) * uact[...]
    spread(fa, hid)
    cross_hid = swap_cols(hid)
    for k in PARTS:
        store(hid[k].at[:, pl.ds(0, HID)], h_out.at[k], 2)

    def reuse(s, k):
        for j in (1, 2, 3):
            seconds[s][k][j].sent()
            thirds[s][k][j].sent()

    def back3(s, k):
        _, d2, d3 = ROUTES[k]
        out = {}
        for j in (2, 1, 3, 0):
            c2 = at(d2, j)
            here = rows(c2 * 4 + c[d3], 32)
            out[j] = remote.group(crecv[s][k].at[pl.ds(0, 96)])
            for j3 in (2, 1, 3):
                out[j].start(send[s][k].at[rows(at(d3, j3) * 4 + c2, 32)], crecv[s][k].at[here], peer(d3, j3))
            crecv[s][k][here, :] = send[s][k][rows(c[d3] * 4 + c2, 32), :]
        return out

    def back2(s, k, thirds_back):
        d2 = ROUTES[k][1]
        out = remote.group(prec[s][k])
        for j in (2, 1, 3, 0):
            thirds_back[j].arrived()
            group = rows(at(d2, j), 128)
            ag[s][k][group, :] = tn((pickw, pick)[s][k][group, :], crecv[s][k][group, :]).astype(BF)
            if j:
                out.start(ag[s][k].at[group], prec[s][k].at[j - 1], peer(d2, j))
        return out

    def back1(s, k, seconds_back):
        seconds_back.arrived()
        d1, d2, _ = ROUTES[k]
        total = ag[s][k][rows(c[d2], 128), :].astype(F32)
        for j in range(3):
            total = total + prec[s][k][j].astype(F32)
        p1send[s][k][...] = total.astype(BF)
        out = remote.group(p1rec[s][k])
        for j in (2, 1, 3):
            out.start(p1send[s][k].at[rows(at(d1, j), 32)], p1rec[s][k].at[j - 1], peer(d1, j))
        return out

    def back0(s, k, firsts_back, dst):
        firsts_back.arrived()
        total = p1send[s][k][rows(c[ROUTES[k][0]], 32), :].astype(F32)
        for j in range(3):
            total = total + p1rec[s][k][j].astype(F32)
        dst[:, pl.ds(FROM[k], WIDE[k])] = total.astype(BF)

    out3 = []
    for k in PARTS:
        swaps[2][k].arrived()
        cross_hid[k].arrived()
        reuse(0, k)
        send[0][k][...] = nn(hid[k][...], both[2][k][...]).astype(BF)
        out3.append(back3(0, k))

    cross_og = [forward(1, k) for k in PARTS]
    for k in PARTS:
        cross_og[k].arrived()
        keep_rows(1, k, g_out)
        contract(1, 2, k)
    gather_parts(fb)
    gate = gact[...]
    sg = jax.nn.sigmoid(gate)
    qprod = fa[...].astype(BF).astype(F32) * fb[...]
    fa[...] = fb[...] * uact[...] * sg * (1.0 + gate * (1.0 - sg))
    spread(fa, gdel)
    cross_gd = swap_cols(gdel)
    fa[...] = fb[...] * (gate * sg)
    spread(fa, udel)
    cross_ud = swap_cols(udel)
    qbuf[...] = lax.dot_general(
        jnp.ones((8, HID), F32), qprod, (((1,), (1,)), ((), ())), precision=lax.Precision.HIGHEST, preferred_element_type=F32
    )
    cross_q = remote.one(qbuf, qsib, sib)
    for k in PARTS:
        store(gdel[k].at[:, pl.ds(0, HID)], gd_out.at[k], 3)
        store(udel[k].at[:, pl.ds(0, HID)], ud_out.at[k], 4)

    out2 = [back2(0, k, out3[k]) for k in PARTS]

    bk3 = []
    for k in PARTS:
        for w in range(2):
            swaps[w][k].arrived()
        cross_gd[k].arrived()
        cross_ud[k].arrived()
        reuse(1, k)
        send[1][k][...] = (nn(gdel[k][...], both[0][k][...]) + nn(udel[k][...], both[1][k][...])).astype(BF)
        bk3.append(back3(1, k))

    d1, d2, d3 = ROUTES[0]
    cross_q.arrived()
    q = qbuf[...] + qsib[...]
    for i in range(4):
        rgsend[i] = q[:, i * 128 : i * 128 + 128]
    rg3 = remote.group(qrec.at[pl.ds(0, 3)])
    for j in (2, 1, 3):
        rg3.start(rgsend.at[at(d3, j)], qrec.at[c[d3]], peer(d3, j))
    qrec[c[d3]] = rgsend[c[d3]]

    out1 = [back1(0, k, out2[k]) for k in PARTS]

    rg3.arrived()
    rg3.sent()
    for c2 in range(4):
        ids, wts = table(0, c2)
        spots = jnp.concatenate([qrec[d][:, c2 * 32 : c2 * 32 + 32] for d in range(4)], axis=1)
        values = jnp.dot(
            jnp.where(sub8 == lane8, spots, 0.0),
            pick[0][pl.ds(c2 * 128, 128), :].astype(F32),
            precision=lax.Precision.HIGHEST,
            preferred_element_type=F32,
        )
        rg = jnp.zeros((8, 128), F32)
        for d in range(4):
            rg = rg + jnp.where(ids == expert_at(d3, d), values[d : d + 1, :], 0.0)
        rgsend[c2] = rg / wts
    rgc2 = remote.group(rg2)
    for j in (2, 1, 3):
        rgc2.start(rgsend.at[at(d2, j)], rg2.at[j - 1], peer(d2, j))

    bk2 = [back2(1, k, bk3[k]) for k in PARTS]
    rgc2.arrived()
    rg1send[...] = rgsend[c[d2]] + rg2[0] + rg2[1] + rg2[2]
    rgc1 = remote.group(rg1)
    for j in (2, 1, 3):
        rgc1.start(rg1send, rg1.at[j - 1], peer(d1, j))
    for k in PARTS:
        back0(0, k, out1[k], mixed)
    rgc1.arrived()
    rg = rg1send[...] + rg1[0] + rg1[1] + rg1[2]
    mine = rg[:, 0:32]
    for i in range(1, 4):
        mine = jnp.where(c[d1] == i, rg[:, i * 32 : i * 32 + 32], mine)
    rgo[...] = mine
    bk1 = [back1(1, k, bk2[k]) for k in PARTS]
    for i, dst in enumerate((t_out, g_out, h_out, gd_out, ud_out)):
        pltpu.make_async_copy(dst, dst, osems.at[i]).wait()
    for k in PARTS:
        back0(1, k, bk1[k], tgrad)
    remote.finish()


N_GROUPS = 124


def run_main(tok, og, ids, wts, gw, uw, dw):
    vm = pltpu.VMEM
    scratch = [vm((16, 128), F32)]

    def per(make):
        scratch.extend(make(WIDE[k]) for k in PARTS)

    for _ in range(8):
        per(lambda w: vm((512, w), BF))
    per(lambda w: vm((4, 4, 16, 128), F32))
    per(lambda w: vm((512, 128), BF))
    per(lambda w: vm((512, 128), BF))
    per(lambda w: vm((512, 1), F32))
    for _ in range(3):
        per(lambda w: vm((2 * HID, w), BF))
    for _ in range(3):
        per(lambda w: vm((HID, w), BF))
    per(lambda w: vm((512, HID), F32))
    scratch.extend(vm((512, HID), F32) for _ in range(4))
    for _ in range(3):
        per(lambda w: vm((512, 2 * HID), BF))
    scratch.extend(vm(s, F32) for s in ((8, 512), (8, 512), (4, 8, 128), (4, 8, 128), (3, 8, 128), (8, 128), (3, 8, 128)))
    for _ in range(2):
        per(lambda w: vm((512, w), BF))
    for _ in range(2):
        per(lambda w: vm((3, 128, w), BF))
    for _ in range(2):
        per(lambda w: vm((128, w), BF))
    for _ in range(2):
        per(lambda w: vm((3, 32, w), BF))
    scratch.extend(
        [
            pltpu.SemaphoreType.DMA((N_GROUPS,)),
            pltpu.SemaphoreType.DMA((N_GROUPS,)),
            pltpu.SemaphoreType.DMA((3,)),
            pltpu.SemaphoreType.DMA((5,)),
        ]
    )
    in_vmem = pl.BlockSpec(memory_space=pltpu.VMEM)
    anywhere = pl.BlockSpec(memory_space=pl.ANY)
    shape = jax.ShapeDtypeStruct
    return pl.pallas_call(
        main_kernel,
        out_shape=(
            shape((32, HALF), BF),
            shape((32, HALF), BF),
            shape((8, 32), F32),
            shape((512, 2 * HALF), BF),
            shape((512, 2 * HALF), BF),
            shape((3, 512, HID), BF),
            shape((3, 512, HID), BF),
            shape((3, 512, HID), BF),
        ),
        in_specs=[in_vmem] * 4 + [anywhere] * 3,
        out_specs=(in_vmem,) * 3 + (anywhere,) * 5,
        scratch_shapes=scratch,
        compiler_params=pltpu.CompilerParams(collective_id=0, has_side_effects=True, vmem_limit_bytes=63 * 2**20),
        cost_estimate=pl.CostEstimate(flops=10**10, bytes_accessed=2 * 10**7, transcendentals=10**6),
    )(tok, og, ids, wts, gw, uw, dw)


def grads_kernel(t_in, g_in, h_in, gd_in, ud_in, gg, ug, dg, tv, gv, hv, gdv, udv, ggv, ugv, dgv, lsems, csems, osems):
    lefts, pairs = [], []
    for k in PARTS:
        lefts.append(
            [
                pltpu.make_async_copy(src.at[k], dst.at[k], lsems.at[k * 3 + i])
                for i, (src, dst) in enumerate(((gd_in, gdv), (ud_in, udv), (h_in, hv)))
            ]
        )
        for copy in lefts[k]:
            copy.start()
        for half in range(2):
            cols = pl.ds(half * HALF + FROM[k], WIDE[k])
            at = (k * 2 + half) * 2
            pair = [
                pltpu.make_async_copy(t_in.at[:, cols], tv.at[:, cols], csems.at[at]),
                pltpu.make_async_copy(g_in.at[:, cols], gv.at[:, cols], csems.at[at + 1]),
            ]
            for copy in pair:
                copy.start()
            pairs.append(pair)
    outs = []
    for k in PARTS:
        for copy in lefts[k]:
            copy.wait()
        turned = [left[k].T for left in (gdv, udv, hv)]
        for half in range(2):
            cols = pl.ds(half * HALF + FROM[k], WIDE[k])
            for copy in pairs[k * 2 + half]:
                copy.wait()
            for left, right, mid, dst in zip(turned, (tv, tv, gv), (ggv, ugv, dgv), (gg, ug, dg)):
                mid[:, cols] = nn(left, right[:, cols]).astype(BF)
                out = pltpu.make_async_copy(mid.at[:, cols], dst.at[0, :, cols], osems.at[len(outs)])
                out.start()
                outs.append(out)
    for out in outs:
        out.wait()


def run_grads(t_rows, g_rows, h, gd, ud):
    anywhere = pl.BlockSpec(memory_space=pl.ANY)
    vm = pltpu.VMEM
    dma = pltpu.SemaphoreType.DMA
    return pl.pallas_call(
        grads_kernel,
        out_shape=(jax.ShapeDtypeStruct((1, HID, 2 * HALF), BF),) * 3,
        in_specs=[anywhere] * 5,
        out_specs=(anywhere,) * 3,
        scratch_shapes=[vm((512, 2 * HALF), BF)] * 2
        + [vm((3, 512, HID), BF)] * 3
        + [vm((HID, 2 * HALF), BF)] * 3
        + [dma((9,)), dma((12,)), dma((18,))],
        compiler_params=pltpu.CompilerParams(vmem_limit_bytes=62 * 2**20),
        cost_estimate=pl.CostEstimate(flops=5 * 10**9, bytes_accessed=2 * 10**7, transcendentals=0),
    )(t_rows, g_rows, h, gd, ud)


def shards(tokens, route_ids, route_weight, gate_weight, up_weight, down_weight, out_grad):
    mixed, tgrad, rg, t_rows, g_rows, h, gd, ud = run_main(
        tokens, out_grad, route_ids.T, route_weight.T, gate_weight, up_weight, down_weight
    )
    gate_grad, up_grad, down_grad = run_grads(t_rows, g_rows, h, gd, ud)
    return (mixed, tgrad, rg.T, gate_grad, up_grad, down_grad)


def solution(mesh):
    placed = (
        P("expert", "tensor"),
        P("expert", None),
        P("expert", None),
        P("expert", "tensor", None),
        P("expert", "tensor", None),
        P("expert", "tensor", None),
        P("expert", "tensor"),
    )
    return jax.shard_map(
        shards,
        mesh=mesh,
        in_specs=placed,
        out_specs=(
            P("expert", "tensor"),
            P("expert", "tensor"),
            P("expert", None),
            P("expert", "tensor", None),
            P("expert", "tensor", None),
            P("expert", "tensor", None),
        ),
        check_vma=False,
    )
```

time: 134 us -> 117 us (0.87)
  Pallas kernels: 124 us -> 114 us
  local copies, waits for them, and re-layouts: 7.34 us -> 1.92 us
    pallas_call x1, Pallas kernels: 109 us -> 103 us  [run_main(): pl.pallas_call(main_kernel, out_shape=(shape((32, HALF), BF), shape((32,...]
    pallas_call x1, Pallas kernels: 15.1 us -> 10.9 us  [run_grads(): pl.pallas_call(grads_kernel, out_shape=(jax.ShapeDtypeStruct((1, HID, 2 *...]
    unnamed x12 -> x9, local copies, waits for them, and re-layouts: 5.13 us -> 1.92 us
    transpose x1 -> x0, local copies, waits for them, and re-layouts: 1.35 us -> none  [shards(): route_grad = lax.dynamic_slice_in_dim(rg, z * 32, 32, axis=1).T]
where the time goes in v2:
time: 117 us; the launch traced here: 116 us
  Pallas kernels  114 us (97%)
  local copies, waits for them, and re-layouts  1.92 us (2%)
    pallas_call x1, Pallas kernels, run_main(): pl.pallas_call(main_kernel, out_shape=(shape((32, HALF), BF), shape((32,...  103 us
    pallas_call x1, Pallas kernels, run_grads(): pl.pallas_call(grads_kernel, out_shape=(jax.ShapeDtypeStruct((1, HID, 2 *...  10.9 us

profile of v2, /device:TPU:1, one launch (start us, length us, event | category | flops | bytes accessed | tf_op | source)
XLA Modules:
  0.0 116.2 jit_solution(16714480566590510503)
XLA Ops:
  0.6 102.7 %shard_map.118 = (bf16[32,2048]{1,0:T(8,128)(2,1)}, bf16[32,2048]{1,0:T(8,128)(2,1)}, f32[8,32]{1,0:T(8,128)}, bf16[512,4096]{1,0:T(8,128)(2,1)}, bf16[512,4096]...) custom-call(bf16[32,2048]{1,0:T(8,128)(2,1)} %refs_0_.1, ...), custom_call_target="tpu_custom_call" | custom-call | flops 10000000000 | bytes 20000000 | tf_op jit(solution)/shard_map/pallas_call | solution.py:501
  103.3 0.0 copy-start.1
  103.3 0.0 copy-start
  103.3 0.0 copy-start.2
  103.3 10.9 %shard_map.119 = (bf16[1,384,4096]{2,1,0:T(8,128)(2,1)}, bf16[1,384,4096]{2,1,0:T(8,128)(2,1)}, bf16[1,384,4096]{2,1,0:T(8,128)(2,1)}) custom-call(bf16[512,4096]{1,0:T(8,128)(2,1)} %get-tuple-element.20.t_in, bf16[512,4096]{1,0:T(8,128)(2,1)} %get-tuple-element.21.g_in, bf16[3,512,384]{2,1,0:T(8,128)(2,1)} %get-tuple-element.22.h_in, ...), custom_call_target="tpu_custom_call" | custom-call | flops 5000000000 | bytes 20000000 | tf_op jit(solution)/shard_map/pallas_call | solution.py:564
  114.3 0.0 copy-done.1
  114.3 0.7 copy.16
  115.0 0.0 copy-done
  115.0 0.7 copy.17
  115.6 0.0 copy-done.2
  115.6 0.6 copy.18
Async XLA Ops:
  103.3 11.0 %copy-start.1 = (bf16[32,2048]{1,0:T(8,128)(2,1)S(1)}, bf16[32,2048]{1,0:T(8,128)(2,1)}, u32[]{:S(2)}) copy-start(bf16[32,2048]{1,0:T(8,128)(2,1)} %get-tuple-element.34) | copy-start | bytes 393220
  103.3 11.6 %copy-start = (bf16[32,2048]{1,0:T(8,128)(2,1)S(1)}, bf16[32,2048]{1,0:T(8,128)(2,1)}, u32[]{:S(2)}) copy-start(bf16[32,2048]{1,0:T(8,128)(2,1)} %get-tuple-element.35) | copy-start | bytes 393220
  103.3 12.3 %copy-start.2 = (f32[8,32]{1,0:T(8,128)S(1)}, f32[8,32]{1,0:T(8,128)}, u32[]{:S(2)}) copy-start(f32[8,32]{1,0:T(8,128)} %get-tuple-element.19) | copy-start | bytes 3076

commit v3 on v2

--- a/solution.py
+++ b/solution.py
@@ -164,7 +164,17 @@
         first[s][k].arrived()
         d2 = ROUTES[k][1]
         block = ag[s][k].at[rows(c[d2], 128)]
-        return {j: remote.one(block, block, peer(d2, j)) for j in (2, 1, 3)}
+        return {
+            1: remote.one(block, block, peer(d2, 1)),
+            3: remote.one(block, block, peer(d2, 3)),
+            2: remote.group(block),
+        }
+
+    def relay(s, k, j):
+        d2 = ROUTES[k][1]
+        seconds[s][k][j].arrived()
+        half = ag[s][k].at[rows(at(d2, 4 - j) * 2 + j // 2, 64)]
+        seconds[s][k][2].start(half, half, peer(d2, j))
 
     lane16 = lax.broadcasted_iota(jnp.int32, (16, 128), 1) // 32
     tri_r = lax.broadcasted_iota(jnp.int32, (128, 128), 0)
@@ -232,25 +242,27 @@
     for k in PARTS:
         tables(k, c[ROUTES[k][1]])
         third(0, k, 0)
-    for k in PARTS:
-        seconds[1].append(second(1, k))
-    for k in PARTS:
-        third(1, k, 0)
 
     for load in loads:
         load.wait()
     swaps = [[remote.one(rest[w][k], both[w][k].at[pl.ds(HID, HID)], sib) for k in PARTS] for w in range(3)]
 
-    for j in (1, 3, 2):
+    for j in (1, 3):
+        for k in PARTS:
+            relay(0, k, j)
         for k in PARTS:
             second_tab[k][j].arrived()
             tables(k, at(ROUTES[k][1], 4 - j))
-            seconds[0][k][j].arrived()
             third(0, k, 4 - j)
-    for j in (1, 3, 2):
-        for k in PARTS:
-            seconds[1][k][j].arrived()
-            third(1, k, 4 - j)
+    for k in PARTS:
+        seconds[1].append(second(1, k))
+    for k in PARTS:
+        second_tab[k][2].arrived()
+        tables(k, at(ROUTES[k][1], 2))
+        seconds[0][k][2].arrived()
+        third(0, k, 2)
+    for k in PARTS:
+        third(1, k, 0)
 
     def store(src, dst, i):
         pltpu.make_async_copy(src, dst, osems.at[i]).start()
@@ -266,8 +278,11 @@
         d1, d2, d3 = ROUTES[k]
         return pl.ds(pl.multiple_of(((v[d3] * 4 + v[d2]) * 4 + v[d1]) * 8, 8), 8)
 
-    def contract(s, w, k):
-        part[k][...] = nt(own[s][k][...], both[w][k][pl.ds(0, HID), :]) + nt(oth[s][k][...], rest[w][k][...])
+    def contract_own(s, w, k):
+        part[k][...] = nt(own[s][k][...], both[w][k][pl.ds(0, HID), :])
+
+    def contract_oth(s, w, k):
+        part[k][...] += nt(oth[s][k][...], rest[w][k][...])
 
     def gather_parts(dst):
         def body(i, carry):
@@ -280,34 +295,49 @@
 
         lax.fori_loop(0, 16, body, 0)
 
-    def spread(src, dst):
-        dst[0][:, pl.ds(0, HID)] = src[...].astype(BF)
+    def spread(src, dst, k):
+        if k == 0:
+            dst[:, pl.ds(0, HID)] = src[...].astype(BF)
+            return
 
         def body(i, carry):
             a, b = i // 4, i % 4
-            group = rows(i, 32)
-            dst[1][group, pl.ds(0, HID)] = jnp.concatenate([src[spot(0, x, a, b), :] for x in range(4)], axis=0).astype(BF)
-            dst[2][group, pl.ds(0, HID)] = jnp.concatenate([src[spot(0, b, y, a), :] for y in range(4)], axis=0).astype(BF)
+            spots = [spot(0, n, a, b) if k == 1 else spot(0, b, n, a) for n in range(4)]
+            dst[rows(i, 32), pl.ds(0, HID)] = jnp.concatenate([src[at, :] for at in spots], axis=0).astype(BF)
             return carry
 
         lax.fori_loop(0, 16, body, 0)
 
     def swap_cols(dst):
-        return [remote.one(dst[k].at[:, pl.ds(0, HID)], dst[k].at[:, pl.ds(HID, HID)], sib) for k in PARTS]
-
-    cross_tok = [forward(0, k) for k in PARTS]
+        return remote.one(dst.at[:, pl.ds(0, HID)], dst.at[:, pl.ds(HID, HID)], sib)
+
+    cross_tok = []
+    for k in PARTS:
+        cross_tok.append(forward(0, k))
+        contract_own(0, 0, k)
     for k in PARTS:
         cross_tok[k].arrived()
         keep_rows(0, k, t_out)
-        contract(0, 0, k)
+        contract_oth(0, 0, k)
     gather_parts(gact)
-    for k in PARTS:
-        contract(0, 1, k)
+    for j in (1, 3):
+        for k in PARTS:
+            relay(1, k, j)
+        for k in PARTS:
+            third(1, k, 4 - j)
+    for k in PARTS:
+        contract_own(0, 1, k)
+        contract_oth(0, 1, k)
+    for k in PARTS:
+        seconds[1][k][2].arrived()
+        third(1, k, 2)
     gather_parts(uact)
     gate = gact[...]
     fa[...] = gate * jax.nn.sigmoid(gate) * uact[...]
-    spread(fa, hid)
-    cross_hid = swap_cols(hid)
+    cross_hid = []
+    for k in PARTS:
+        spread(fa, hid[k], k)
+        cross_hid.append(swap_cols(hid[k]))
     for k in PARTS:
         store(hid[k].at[:, pl.ds(0, HID)], h_out.at[k], 2)
 
@@ -328,15 +358,16 @@
             crecv[s][k][here, :] = send[s][k][rows(c[d3] * 4 + c2, 32), :]
         return out
 
-    def back2(s, k, thirds_back):
-        d2 = ROUTES[k][1]
-        out = remote.group(prec[s][k])
+    def back2(s, thirds_back):
+        out = [remote.group(prec[s][k]) for k in PARTS]
         for j in (2, 1, 3, 0):
-            thirds_back[j].arrived()
-            group = rows(at(d2, j), 128)
-            ag[s][k][group, :] = tn((pickw, pick)[s][k][group, :], crecv[s][k][group, :]).astype(BF)
-            if j:
-                out.start(ag[s][k].at[group], prec[s][k].at[j - 1], peer(d2, j))
+            for k in PARTS:
+                d2 = ROUTES[k][1]
+                thirds_back[k][j].arrived()
+                group = rows(at(d2, j), 128)
+                ag[s][k][group, :] = tn((pickw, pick)[s][k][group, :], crecv[s][k][group, :]).astype(BF)
+                if j:
+                    out[k].start(ag[s][k].at[group], prec[s][k].at[j - 1], peer(d2, j))
         return out
 
     def back1(s, k, seconds_back):
@@ -366,21 +397,27 @@
         send[0][k][...] = nn(hid[k][...], both[2][k][...]).astype(BF)
         out3.append(back3(0, k))
 
-    cross_og = [forward(1, k) for k in PARTS]
+    cross_og = []
+    for k in PARTS:
+        cross_og.append(forward(1, k))
+        contract_own(1, 2, k)
     for k in PARTS:
         cross_og[k].arrived()
         keep_rows(1, k, g_out)
-        contract(1, 2, k)
+        contract_oth(1, 2, k)
     gather_parts(fb)
     gate = gact[...]
     sg = jax.nn.sigmoid(gate)
-    qprod = fa[...].astype(BF).astype(F32) * fb[...]
-    fa[...] = fb[...] * uact[...] * sg * (1.0 + gate * (1.0 - sg))
-    spread(fa, gdel)
-    cross_gd = swap_cols(gdel)
-    fa[...] = fb[...] * (gate * sg)
-    spread(fa, udel)
-    cross_ud = swap_cols(udel)
+    grad = fb[...]
+    qprod = fa[...].astype(BF).astype(F32) * grad
+    fa[...] = grad * uact[...] * sg * (1.0 + gate * (1.0 - sg))
+    fb[...] = grad * (gate * sg)
+    cross_gd, cross_ud = [], []
+    for k in PARTS:
+        spread(fa, gdel[k], k)
+        cross_gd.append(swap_cols(gdel[k]))
+        spread(fb, udel[k], k)
+        cross_ud.append(swap_cols(udel[k]))
     qbuf[...] = lax.dot_general(
         jnp.ones((8, HID), F32), qprod, (((1,), (1,)), ((), ())), precision=lax.Precision.HIGHEST, preferred_element_type=F32
     )
@@ -389,7 +426,7 @@
         store(gdel[k].at[:, pl.ds(0, HID)], gd_out.at[k], 3)
         store(udel[k].at[:, pl.ds(0, HID)], ud_out.at[k], 4)
 
-    out2 = [back2(0, k, out3[k]) for k in PARTS]
+    out2 = back2(0, out3)
 
     bk3 = []
     for k in PARTS:
@@ -432,7 +469,7 @@
     for j in (2, 1, 3):
         rgc2.start(rgsend.at[at(d2, j)], rg2.at[j - 1], peer(d2, j))
 
-    bk2 = [back2(1, k, bk3[k]) for k in PARTS]
+    bk2 = back2(1, bk3)
     rgc2.arrived()
     rg1send[...] = rgsend[c[d2]] + rg2[0] + rg2[1] + rg2[2]
     rgc1 = remote.group(rg1)
@@ -518,7 +555,15 @@
     )(tok, og, ids, wts, gw, uw, dw)
 
 
-def grads_kernel(t_in, g_in, h_in, gd_in, ud_in, gg, ug, dg, tv, gv, hv, gdv, udv, ggv, ugv, dgv, lsems, csems, osems):
+def grads_kernel(
+    t_in, g_in, h_in, gd_in, ud_in, mixed_in, tgrad_in, rg_in,
+    gg, ug, dg, mixed, tgrad, rg,
+    tv, gv, hv, gdv, udv, ggv, ugv, dgv, lsems, csems, osems, psems
+):
+    passing = [
+        pltpu.make_async_copy(src, dst, psems.at[i])
+        for i, (src, dst) in enumerate(((mixed_in, mixed), (tgrad_in, tgrad), (rg_in, rg)))
+    ]
     lefts, pairs = [], []
     for k in PARTS:
         lefts.append(
@@ -539,47 +584,55 @@
             for copy in pair:
                 copy.start()
             pairs.append(pair)
+    for copy in passing:
+        copy.start()
     outs = []
     for k in PARTS:
         for copy in lefts[k]:
             copy.wait()
-        turned = [left[k].T for left in (gdv, udv, hv)]
+        pair_t = jnp.concatenate([gdv[k].T, udv[k].T], axis=0)
+        hid_t = hv[k].T
         for half in range(2):
             cols = pl.ds(half * HALF + FROM[k], WIDE[k])
             for copy in pairs[k * 2 + half]:
                 copy.wait()
-            for left, right, mid, dst in zip(turned, (tv, tv, gv), (ggv, ugv, dgv), (gg, ug, dg)):
-                mid[:, cols] = nn(left, right[:, cols]).astype(BF)
+            two = nn(pair_t, tv[:, cols]).astype(BF)
+            ggv[:, cols] = two[:HID]
+            ugv[:, cols] = two[HID:]
+            dgv[:, cols] = nn(hid_t, gv[:, cols]).astype(BF)
+            for mid, dst in zip((ggv, ugv, dgv), (gg, ug, dg)):
                 out = pltpu.make_async_copy(mid.at[:, cols], dst.at[0, :, cols], osems.at[len(outs)])
                 out.start()
                 outs.append(out)
-    for out in outs:
+    for out in outs + passing:
         out.wait()
 
 
-def run_grads(t_rows, g_rows, h, gd, ud):
+def run_grads(t_rows, g_rows, h, gd, ud, mixed, tgrad, rg):
     anywhere = pl.BlockSpec(memory_space=pl.ANY)
     vm = pltpu.VMEM
     dma = pltpu.SemaphoreType.DMA
+    shape = jax.ShapeDtypeStruct
     return pl.pallas_call(
         grads_kernel,
-        out_shape=(jax.ShapeDtypeStruct((1, HID, 2 * HALF), BF),) * 3,
-        in_specs=[anywhere] * 5,
-        out_specs=(anywhere,) * 3,
+        out_shape=(shape((1, HID, 2 * HALF), BF),) * 3
+        + tuple(shape(x.shape, x.dtype) for x in (mixed, tgrad, rg)),
+        in_specs=[anywhere] * 8,
+        out_specs=(anywhere,) * 6,
         scratch_shapes=[vm((512, 2 * HALF), BF)] * 2
         + [vm((3, 512, HID), BF)] * 3
         + [vm((HID, 2 * HALF), BF)] * 3
-        + [dma((9,)), dma((12,)), dma((18,))],
+        + [dma((9,)), dma((12,)), dma((18,)), dma((3,))],
         compiler_params=pltpu.CompilerParams(vmem_limit_bytes=62 * 2**20),
         cost_estimate=pl.CostEstimate(flops=5 * 10**9, bytes_accessed=2 * 10**7, transcendentals=0),
-    )(t_rows, g_rows, h, gd, ud)
+    )(t_rows, g_rows, h, gd, ud, mixed, tgrad, rg)
 
 
 def shards(tokens, route_ids, route_weight, gate_weight, up_weight, down_weight, out_grad):
     mixed, tgrad, rg, t_rows, g_rows, h, gd, ud = run_main(
         tokens, out_grad, route_ids.T, route_weight.T, gate_weight, up_weight, down_weight
     )
-    gate_grad, up_grad, down_grad = run_grads(t_rows, g_rows, h, gd, ud)
+    gate_grad, up_grad, down_grad, mixed, tgrad, rg = run_grads(t_rows, g_rows, h, gd, ud, mixed, tgrad, rg)
     return (mixed, tgrad, rg.T, gate_grad, up_grad, down_grad)
 
 

time: 117 us -> 110 us (0.940)
  Pallas kernels: 114 us -> 109 us
  local copies, waits for them, and re-layouts: 1.92 us -> 0 us
    pallas_call x1, Pallas kernels: 103 us -> 98.1 us  [run_main(): pl.pallas_call(main_kernel, out_shape=(shape((32, HALF), BF), shape((32,...]
    unnamed x9 -> x0, local copies, waits for them, and re-layouts: 1.92 us -> none
where the time goes in v3:
time: 110 us
  Pallas kernels  109 us (99%)
    pallas_call x1, Pallas kernels, run_main(): pl.pallas_call(main_kernel, out_shape=(shape((32, HALF), BF), shape((32,...  98.1 us
    pallas_call x1, Pallas kernels, run_grads(): pl.pallas_call(grads_kernel, out_shape=(shape((1, HID, 2 * HALF), BF),) *...  11 us

profile of v3, /device:TPU:1, one launch (start us, length us, event | category | flops | bytes accessed | tf_op | source)
XLA Modules:
  0.0 109.9 jit_solution(16798502980835409256)
XLA Ops:
  0.6 98.1 %shard_map.118 = (bf16[32,2048]{1,0:T(8,128)(2,1)}, bf16[32,2048]{1,0:T(8,128)(2,1)}, f32[8,32]{1,0:T(8,128)}, bf16[512,4096]{1,0:T(8,128)(2,1)}, bf16[512,4096]...) custom-call(bf16[32,2048]{1,0:T(8,128)(2,1)} %refs_0_.1, ...), custom_call_target="tpu_custom_call" | custom-call | flops 10000000000 | bytes 20000000 | tf_op jit(solution)/shard_map/pallas_call | solution.py:538
  98.7 11.0 %shard_map.119 = (bf16[1,384,4096]{2,1,0:T(8,128)(2,1)}, bf16[1,384,4096]{2,1,0:T(8,128)(2,1)}, bf16[1,384,4096]{2,1,0:T(8,128)(2,1)}, bf16[32,2048]{1,0:T(8,128...) custom-call(bf16[512,4096]{1,0:T(8,128)(2,1)} %get-tuple-element.20.t_in, bf16[512,4096]{1,0:T(8,128)(2,1)} %get-tuple-element.21.g_in, ...), custom_call_target="tpu_custom_call" | custom-call | flops 5000000000 | bytes 20000000 | tf_op jit(solution)/shard_map/pallas_call | solution.py:616

commit v4 on v3

--- a/solution.py
+++ b/solution.py
@@ -84,7 +84,8 @@
     send = [take(3), take(3)]
     own = [take(3), take(3)]
     oth = [take(3), take(3)]
-    tabs = take(3)
+    (tabs_all,) = take(1)
+    tabs = [tabs_all.at[k] for k in PARTS]
     pick = take(3)
     pickw = take(3)
     wcol = take(3)
@@ -145,12 +146,11 @@
     pl.semaphore_wait(barrier, 10)
 
     first = [[], []]
-    first_tab = []
+    first_tab = remote.group(tabs_all.at[:, 0, pl.ds(0, 3)])
     for k in PARTS:
         d1, d2, _ = ROUTES[k]
-        first_tab.append(remote.group(tabs[k].at[0, pl.ds(0, 3)]))
         for j in (2, 1, 3):
-            first_tab[k].start(tab, tabs[k].at[c[d2], c[d1]], peer(d1, j))
+            first_tab.start(tab, tabs[k].at[c[d2], c[d1]], peer(d1, j))
     for s, src in enumerate((tok, og)):
         for k in PARTS:
             d1, d2, _ = ROUTES[k]
@@ -232,11 +232,13 @@
         return out
 
     thirds = [[{j3: remote.group(own[s][k].at[pl.ds(0, 128)]) for j3 in (1, 2, 3)} for k in PARTS] for s in range(2)]
-    seconds, second_tab = [[], []], []
-    for k in PARTS:
-        first_tab[k].arrived()
+    seconds = [[], []]
+    second_tab = {j: remote.group(tabs_all.at[:, 0]) for j in (2, 1, 3)}
+    first_tab.arrived()
+    for k in PARTS:
         d2 = ROUTES[k][1]
-        second_tab.append({j: remote.one(tabs[k].at[c[d2]], tabs[k].at[c[d2]], peer(d2, j)) for j in (2, 1, 3)})
+        for j in (2, 1, 3):
+            second_tab[j].start(tabs[k].at[c[d2]], tabs[k].at[c[d2]], peer(d2, j))
     for k in PARTS:
         seconds[0].append(second(0, k))
     for k in PARTS:
@@ -250,14 +252,14 @@
     for j in (1, 3):
         for k in PARTS:
             relay(0, k, j)
+        second_tab[j].arrived()
         for k in PARTS:
-            second_tab[k][j].arrived()
             tables(k, at(ROUTES[k][1], 4 - j))
             third(0, k, 4 - j)
     for k in PARTS:
         seconds[1].append(second(1, k))
-    for k in PARTS:
-        second_tab[k][2].arrived()
+    second_tab[2].arrived()
+    for k in PARTS:
         tables(k, at(ROUTES[k][1], 2))
         seconds[0][k][2].arrived()
         third(0, k, 2)
@@ -315,6 +317,9 @@
     for k in PARTS:
         cross_tok.append(forward(0, k))
         contract_own(0, 0, k)
+    for j in (1, 3):
+        for k in PARTS:
+            relay(1, k, j)
     for k in PARTS:
         cross_tok[k].arrived()
         keep_rows(0, k, t_out)
@@ -322,15 +327,10 @@
     gather_parts(gact)
     for j in (1, 3):
         for k in PARTS:
-            relay(1, k, j)
-        for k in PARTS:
             third(1, k, 4 - j)
     for k in PARTS:
         contract_own(0, 1, k)
         contract_oth(0, 1, k)
-    for k in PARTS:
-        seconds[1][k][2].arrived()
-        third(1, k, 2)
     gather_parts(uact)
     gate = gact[...]
     fa[...] = gate * jax.nn.sigmoid(gate) * uact[...]
@@ -341,29 +341,30 @@
     for k in PARTS:
         store(hid[k].at[:, pl.ds(0, HID)], h_out.at[k], 2)
 
+    for k in PARTS:
+        seconds[1][k][2].arrived()
+        third(1, k, 2)
+
     def reuse(s, k):
         for j in (1, 2, 3):
             seconds[s][k][j].sent()
             thirds[s][k][j].sent()
 
-    def back3(s, k):
+    def back3(s, k, out):
         _, d2, d3 = ROUTES[k]
-        out = {}
         for j in (2, 1, 3, 0):
             c2 = at(d2, j)
             here = rows(c2 * 4 + c[d3], 32)
-            out[j] = remote.group(crecv[s][k].at[pl.ds(0, 96)])
             for j3 in (2, 1, 3):
                 out[j].start(send[s][k].at[rows(at(d3, j3) * 4 + c2, 32)], crecv[s][k].at[here], peer(d3, j3))
             crecv[s][k][here, :] = send[s][k][rows(c[d3] * 4 + c2, 32), :]
-        return out
 
     def back2(s, thirds_back):
         out = [remote.group(prec[s][k]) for k in PARTS]
         for j in (2, 1, 3, 0):
+            thirds_back[j].arrived()
             for k in PARTS:
                 d2 = ROUTES[k][1]
-                thirds_back[k][j].arrived()
                 group = rows(at(d2, j), 128)
                 ag[s][k][group, :] = tn((pickw, pick)[s][k][group, :], crecv[s][k][group, :]).astype(BF)
                 if j:
@@ -389,13 +390,13 @@
             total = total + p1rec[s][k][j].astype(F32)
         dst[:, pl.ds(FROM[k], WIDE[k])] = total.astype(BF)
 
-    out3 = []
+    out3 = {j: remote.group(gw.at[0, pl.ds(0, 96), pl.ds(0, HALF)]) for j in (2, 1, 3, 0)}
     for k in PARTS:
         swaps[2][k].arrived()
         cross_hid[k].arrived()
         reuse(0, k)
         send[0][k][...] = nn(hid[k][...], both[2][k][...]).astype(BF)
-        out3.append(back3(0, k))
+        back3(0, k, out3)
 
     cross_og = []
     for k in PARTS:
@@ -428,7 +429,7 @@
 
     out2 = back2(0, out3)
 
-    bk3 = []
+    bk3 = {j: remote.group(gw.at[0, pl.ds(0, 96), pl.ds(0, HALF)]) for j in (2, 1, 3, 0)}
     for k in PARTS:
         for w in range(2):
             swaps[w][k].arrived()
@@ -436,7 +437,7 @@
         cross_ud[k].arrived()
         reuse(1, k)
         send[1][k][...] = (nn(gdel[k][...], both[0][k][...]) + nn(udel[k][...], both[1][k][...])).astype(BF)
-        bk3.append(back3(1, k))
+        back3(1, k, bk3)
 
     d1, d2, d3 = ROUTES[0]
     cross_q.arrived()
@@ -491,7 +492,7 @@
     remote.finish()
 
 
-N_GROUPS = 124
+N_GROUPS = 94
 
 
 def run_main(tok, og, ids, wts, gw, uw, dw):
@@ -503,7 +504,7 @@
 
     for _ in range(8):
         per(lambda w: vm((512, w), BF))
-    per(lambda w: vm((4, 4, 16, 128), F32))
+    scratch.append(vm((3, 4, 4, 16, 128), F32))
     per(lambda w: vm((512, 128), BF))
     per(lambda w: vm((512, 128), BF))
     per(lambda w: vm((512, 1), F32))

time: 110 us -> 107 us (0.973)
  Pallas kernels: 109 us -> 106 us
    pallas_call x1, Pallas kernels: 98.1 us -> 95 us  [run_main(): pl.pallas_call(main_kernel, out_shape=(shape((32, HALF), BF), shape((32,...]
where the time goes in v4:
time: 107 us
  Pallas kernels  106 us (99%)
    pallas_call x1, Pallas kernels, run_main(): pl.pallas_call(main_kernel, out_shape=(shape((32, HALF), BF), shape((32,...  95 us
    pallas_call x1, Pallas kernels, run_grads(): pl.pallas_call(grads_kernel, out_shape=(shape((1, HID, 2 * HALF), BF),) *...  11 us

profile of v4, /device:TPU:1, one launch (start us, length us, event | category | flops | bytes accessed | tf_op | source)
XLA Modules:
  0.0 106.8 jit_solution(13002074047170485968)
XLA Ops:
  0.6 95.0 %shard_map.118 = (bf16[32,2048]{1,0:T(8,128)(2,1)}, bf16[32,2048]{1,0:T(8,128)(2,1)}, f32[8,32]{1,0:T(8,128)}, bf16[512,4096]{1,0:T(8,128)(2,1)}, bf16[512,4096]...) custom-call(bf16[32,2048]{1,0:T(8,128)(2,1)} %refs_0_.1, ...), custom_call_target="tpu_custom_call" | custom-call | flops 10000000000 | bytes 20000000 | tf_op jit(solution)/shard_map/pallas_call | solution.py:539
  95.7 11.0 %shard_map.119 = (bf16[1,384,4096]{2,1,0:T(8,128)(2,1)}, bf16[1,384,4096]{2,1,0:T(8,128)(2,1)}, bf16[1,384,4096]{2,1,0:T(8,128)(2,1)}, bf16[32,2048]{1,0:T(8,128...) custom-call(bf16[512,4096]{1,0:T(8,128)(2,1)} %get-tuple-element.20.t_in, bf16[512,4096]{1,0:T(8,128)(2,1)} %get-tuple-element.21.g_in, ...), custom_call_target="tpu_custom_call" | custom-call | flops 5000000000 | bytes 20000000 | tf_op jit(solution)/shard_map/pallas_call | solution.py:617
